TPU v7x, 32 devices: a whole 2x2x4 slice. The times are simulated.
32 devices in a mesh: expert: 8 (over y, x, core), shard: 4 (over z).
Axes of the slice: x: 2, y: 2, z: 4, core: 2. Of those that a mesh axis runs over, the one named last changes fastest.
Arguments:
- block_in: bfloat16 [4096, 2048], P(('expert', 'shard')), may hold values from -6 to 6
- cotangent: bfloat16 [4096, 2048], P(('expert', 'shard')), may hold values from -6 to 6
- doc_ids: int32 [8, 512], P('expert'), may hold values from 0 to 2, never falling along the last dimension, each value on 1 to 384 neighbouring positions
- routes: int32 [4096, 6], P(('expert', 'shard')), may hold values from 0 to 15, all different within a row; in each aligned block of 128 rows (0 to 127, 128 to 255, ...) at most 64 rows name the same one
- attn_gain: bfloat16 [2048], P('shard'), may hold values from 0.25 to 1.75
- query_weight: bfloat16 [2048, 3072], P('shard'), may hold values from -1 to 1
- kv_down_weight: bfloat16 [2048, 576], P('shard'), may hold values from -0.125 to 0.125
- kv_gain: bfloat16 [512], P('shard'), may hold values from 0.25 to 1.75
- kv_up_weight: bfloat16 [512, 4096], P('shard'), may hold values from -0.25 to 0.25
- out_weight: bfloat16 [2048, 2048], P('shard'), may hold values from -1 to 1
- ffn_gain: bfloat16 [2048], P('shard'), may hold values from 0.25 to 1.75
- router_weight: bfloat16 [2048, 16], P('shard'), may hold values from -1 to 1
- shared_in: bfloat16 [2048, 5632], P('shard'), may hold values from -0.125 to 0.125
- shared_down: bfloat16 [2816, 2048], P('shard'), may hold values from -0.21875 to 0.21875
- expert_in: bfloat16 [16, 4096, 1408], P('expert', None, 'shard'), may hold values from -0.125 to 0.125
- expert_down: bfloat16 [16, 2048, 1408], P('expert', None, 'shard'), may hold values from -0.3125 to 0.3125
Outputs:
- block_out: float32 [4096, 2048], P(('expert', 'shard'))
- input_grad: float32 [4096, 2048], P(('expert', 'shard'))
- attn_gain_grad: float32 [2048], P(('expert', 'shard'))
- query_weight_grad: float32 [2048, 3072], P(('expert', 'shard'))
- kv_down_weight_grad: float32 [2048, 576], P(('expert', 'shard'))
- kv_gain_grad: float32 [512], P(('expert', 'shard'))
- kv_up_weight_grad: float32 [512, 4096], P(('expert', 'shard'))
- out_weight_grad: float32 [2048, 2048], P(('expert', 'shard'))
- ffn_gain_grad: float32 [2048], P(('expert', 'shard'))
- router_weight_grad: float32 [2048, 16], P(('expert', 'shard'))
- shared_in_grad: float32 [2048, 5632], P(('expert', 'shard'))
- shared_down_grad: float32 [2816, 2048], P(('expert', 'shard'))
- expert_in_grad: float32 [16, 4096, 1408], P('expert', None, 'shard')
- expert_down_grad: float32 [16, 2048, 1408], P('expert', None, 'shard')
Inputs may be any that keep to these rules, and one draw needn't show every extreme that they name: `routes`: within the rows of one device (128 tokens) every expert is named at most 64 times. `doc_ids`: in each group the document numbers never fall and run through 0 to 2; a document has 1 to 384 tokens and one has exactly 384.
All inputs are finite; a program needn't handle non-finite values.
Results may differ from a plain program's by a relative error of at most 0.02.
Values may be sent and summed in bfloat16 or wider, within the bound.
A program may use at most 512 MiB of HBM per device.

v0:
```python
import jax
import jax.numpy as jnp
from jax import lax
from jax.sharding import PartitionSpec as P

D = 2048
HEADS = 16
NOPE = 128
ROPE = 64
VDIM = 128
KV_RANK = 512
SH_FF = 2816
TOP = 6
EXP_DEV = 2


EPS = 1e-06
ROPE_BASE = 10000.0


def inv_rms(values):
    return lax.rsqrt(jnp.mean(values * values, axis=-1, keepdims=True) + EPS)


def norm_back(grad_out, values, inv_scale, gain_row):
    scaled = grad_out * gain_row
    grad_in = inv_scale * scaled - values * inv_scale**3 * jnp.mean(
        scaled * values, axis=-1, keepdims=True
    )
    grad_gain = jnp.sum(grad_out * values * inv_scale, axis=0)
    return (grad_in, grad_gain)


def silu_parts(pre_act):
    sigmoid_val = jax.nn.sigmoid(pre_act)
    return (pre_act * sigmoid_val, sigmoid_val * (1.0 + pre_act * (1.0 - sigmoid_val)))


def doc_positions(doc_row):
    index_row = jnp.arange(doc_row.shape[0], dtype=jnp.int32)
    starts = jnp.concatenate([jnp.ones((1,), dtype=bool), doc_row[1:] != doc_row[:-1]])
    begin_at = lax.cummax(jnp.where(starts, index_row, 0), axis=0)
    return index_row - begin_at


def rope_tables(positions):
    half_width = ROPE // 2
    frequency = ROPE_BASE ** (-jnp.arange(half_width, dtype=jnp.float32) / half_width)
    angles = positions.astype(jnp.float32)[:, None] * frequency[None, :]
    return (jnp.cos(angles), jnp.sin(angles))


def rotate(values, cosine, sine_table):
    half_width = cosine.shape[-1]
    front_half = values[..., :half_width]
    back_half = values[..., half_width:]
    return jnp.concatenate(
        [
            front_half * cosine - back_half * sine_table,
            back_half * cosine + front_half * sine_table,
        ],
        axis=-1,
    )


def unrotate(values, cosine, sine_table):
    half_width = cosine.shape[-1]
    front_half = values[..., :half_width]
    back_half = values[..., half_width:]
    return jnp.concatenate(
        [
            front_half * cosine + back_half * sine_table,
            back_half * cosine - front_half * sine_table,
        ],
        axis=-1,
    )


def attention_scores(queries, key_nope, key_rope, allowed):
    score_scale = (NOPE + ROPE) ** (-0.5)
    raw_scores = jnp.einsum(
        "qhd,khd->hqk", queries[..., :NOPE], key_nope, preferred_element_type=jnp.float32
    )
    raw_scores = raw_scores + jnp.einsum(
        "qhd,kd->hqk", queries[..., NOPE:], key_rope, preferred_element_type=jnp.float32
    )
    return jnp.where(allowed[None, :, :], raw_scores * score_scale, -jnp.inf)


def expert_forward(rows_in, gate_w, up_w, down_w):
    gate_pre = jnp.einsum("ecd,edf->ecf", rows_in, gate_w, preferred_element_type=jnp.float32)
    up_pre = jnp.einsum("ecd,edf->ecf", rows_in, up_w, preferred_element_type=jnp.float32)
    gate_act, gate_slope = silu_parts(gate_pre)
    expert_mid = (gate_act * up_pre).astype(jnp.bfloat16)
    partial_value = jnp.einsum(
        "ecf,edf->ecd", expert_mid, down_w, preferred_element_type=jnp.float32
    )
    return (gate_act, gate_slope, up_pre, expert_mid, partial_value)


def expert_backward(
    rows_in, grad_rows, gate_act, gate_slope, up_pre, expert_mid, gate_w, up_w, down_w
):
    down_grad = jnp.einsum(
        "ecd,ecf->edf", grad_rows, expert_mid, preferred_element_type=jnp.float32
    )
    mid_grad = jnp.einsum("ecd,edf->ecf", grad_rows, down_w, preferred_element_type=jnp.float32)
    gate_grad = (mid_grad * up_pre * gate_slope).astype(jnp.bfloat16)
    up_grad = (mid_grad * gate_act).astype(jnp.bfloat16)
    in_grad = jnp.concatenate(
        [
            jnp.einsum("ecd,ecf->edf", rows_in, gate_grad, preferred_element_type=jnp.float32),
            jnp.einsum("ecd,ecf->edf", rows_in, up_grad, preferred_element_type=jnp.float32),
        ],
        axis=1,
    )
    back_part = jnp.einsum(
        "ecf,edf->ecd", gate_grad, gate_w, preferred_element_type=jnp.float32
    ) + jnp.einsum("ecf,edf->ecd", up_grad, up_w, preferred_element_type=jnp.float32)
    return (in_grad, down_grad, back_part)


def local(
    block_in,
    cotangent,
    doc_ids,
    routes,
    attn_gain,
    query_weight,
    kv_down_weight,
    kv_gain,
    kv_up_weight,
    out_weight,
    ffn_gain,
    router_weight,
    shared_in,
    shared_down,
    expert_in,
    expert_down,
):
    tok_dev = block_in.shape[0]
    doc_row = doc_ids[0]
    group_tok = doc_row.shape[0]
    first_row = lax.axis_index("shard") * tok_dev
    experts_all = EXP_DEV * lax.axis_size("expert")
    capacity = tok_dev * TOP * 4 // (3 * experts_all)
    score_scale = (NOPE + ROPE) ** (-0.5)
    (
        gain_attn,
        query_proj,
        kv_down_proj,
        gain_kv,
        kv_up_proj,
        out_proj,
        gain_ffn,
        router_proj,
        shared_in_full,
        shared_down_full,
    ) = (
        lax.all_gather(attn_gain, "shard", axis=0, tiled=True),
        lax.all_gather(query_weight, "shard", axis=0, tiled=True),
        lax.all_gather(kv_down_weight, "shard", axis=0, tiled=True),
        lax.all_gather(kv_gain, "shard", axis=0, tiled=True),
        lax.all_gather(kv_up_weight, "shard", axis=0, tiled=True),
        lax.all_gather(out_weight, "shard", axis=0, tiled=True),
        lax.all_gather(ffn_gain, "shard", axis=0, tiled=True),
        lax.all_gather(router_weight, "shard", axis=0, tiled=True),
        lax.all_gather(shared_in, "shard", axis=0, tiled=True),
        lax.all_gather(shared_down, "shard", axis=0, tiled=True),
    )
    cos_all, sin_all = rope_tables(doc_positions(doc_row))
    cos_own = lax.dynamic_slice_in_dim(cos_all, first_row, tok_dev, 0)
    sin_own = lax.dynamic_slice_in_dim(sin_all, first_row, tok_dev, 0)
    doc_own = lax.dynamic_slice_in_dim(doc_row, first_row, tok_dev, 0)
    query_index = first_row + jnp.arange(tok_dev, dtype=jnp.int32)
    key_index = jnp.arange(group_tok, dtype=jnp.int32)
    allowed = (doc_own[:, None] == doc_row[None, :]) & (key_index[None, :] <= query_index[:, None])
    x_float = block_in.astype(jnp.float32)
    scale_in = inv_rms(x_float)
    x_norm = (x_float * scale_in * gain_attn).astype(jnp.bfloat16)
    query_raw = jnp.dot(x_norm, query_proj, preferred_element_type=jnp.float32).reshape(
        tok_dev, HEADS, NOPE + ROPE
    )
    queries = jnp.concatenate(
        [
            query_raw[..., :NOPE],
            rotate(query_raw[..., NOPE:], cos_own[:, None, :], sin_own[:, None, :]),
        ],
        axis=-1,
    ).astype(jnp.bfloat16)
    latent_raw = jnp.dot(x_norm, kv_down_proj, preferred_element_type=jnp.float32)
    compressed = latent_raw[:, :KV_RANK]
    scale_kv = inv_rms(compressed)
    latent = jnp.concatenate(
        [compressed * scale_kv * gain_kv, rotate(latent_raw[:, KV_RANK:], cos_own, sin_own)],
        axis=-1,
    ).astype(jnp.bfloat16)
    group_latent = lax.all_gather(latent, "shard", axis=0, tiled=True)
    key_rope = group_latent[:, KV_RANK:]
    expanded = (
        jnp.dot(group_latent[:, :KV_RANK], kv_up_proj, preferred_element_type=jnp.float32)
        .astype(jnp.bfloat16)
        .reshape(group_tok, HEADS, NOPE + VDIM)
    )
    key_nope = expanded[..., :NOPE]
    values_all = expanded[..., NOPE:]
    scores = attention_scores(queries, key_nope, key_rope, allowed)
    row_max = jnp.max(scores, axis=-1, keepdims=True)
    lse_rows = row_max + jnp.log(jnp.sum(jnp.exp(scores - row_max), axis=-1, keepdims=True))
    probs_low = jnp.exp(scores - lse_rows).astype(jnp.bfloat16)
    attended = (
        jnp.einsum("hqk,khd->qhd", probs_low, values_all, preferred_element_type=jnp.float32)
        .astype(jnp.bfloat16)
        .reshape(tok_dev, HEADS * VDIM)
    )
    resid = x_float + jnp.dot(attended, out_proj, preferred_element_type=jnp.float32)
    scale_ffn = inv_rms(resid)
    h_norm = (resid * scale_ffn * gain_ffn).astype(jnp.bfloat16)
    logits = jnp.dot(h_norm, router_proj, preferred_element_type=jnp.float32)
    expert_ids = jnp.arange(experts_all, dtype=jnp.int32)
    route_hot = (routes[:, :, None] == expert_ids[None, None, :]).astype(jnp.float32)
    chosen = jnp.sum(route_hot * logits[:, None, :], axis=-1)
    route_weights = jax.nn.softmax(chosen, axis=-1)
    shared_pre = jnp.dot(h_norm, shared_in_full, preferred_element_type=jnp.float32)
    shared_act, shared_slope = silu_parts(shared_pre[:, :SH_FF])
    shared_mid = (shared_act * shared_pre[:, SH_FF:]).astype(jnp.bfloat16)
    shared_out = jnp.dot(shared_mid, shared_down_full, preferred_element_type=jnp.float32)
    flat_count = tok_dev * TOP
    route_flat = routes.reshape(flat_count)
    flat_hot = (route_flat[:, None] == expert_ids[None, :]).astype(jnp.int32)
    slot_rank = jnp.sum((jnp.cumsum(flat_hot, axis=0) - 1) * flat_hot, axis=1)
    slot_index = route_flat * capacity + slot_rank
    owner_row = (
        jnp.full((experts_all * capacity,), flat_count, dtype=jnp.int32)
        .at[slot_index]
        .set(jnp.arange(flat_count, dtype=jnp.int32))
    )
    token_row = owner_row // TOP
    norm_ext = jnp.concatenate([h_norm, jnp.zeros((1, D), jnp.bfloat16)], axis=0)
    send_rows = norm_ext[token_row].reshape(experts_all, capacity, D)
    received = lax.all_to_all(send_rows, "expert", split_axis=0, concat_axis=1, tiled=True)
    rows_all = lax.all_gather(received, "shard", axis=1, tiled=True)
    gate_w = expert_in[:, :D]
    up_w = expert_in[:, D:]
    gate_act, gate_slope, up_pre, expert_mid, partial_value = expert_forward(
        rows_all, gate_w, up_w, expert_down
    )
    result_low = lax.psum_scatter(
        partial_value.astype(jnp.bfloat16), "shard", scatter_dimension=1, tiled=True
    )
    returned = lax.all_to_all(result_low, "expert", split_axis=1, concat_axis=0, tiled=True)
    expert_out = returned.reshape(experts_all * capacity, D)[slot_index].reshape(tok_dev, TOP, D)
    expert_float = expert_out.astype(jnp.float32)
    routed = jnp.sum(route_weights[:, :, None] * expert_float, axis=1)
    block_out = resid + shared_out + routed
    cot_float = cotangent.astype(jnp.float32)
    shared_down_grad = jnp.dot(shared_mid.T, cotangent, preferred_element_type=jnp.float32)
    mid_back = jnp.dot(cotangent, shared_down_full.T, preferred_element_type=jnp.float32)
    shared_pre_grad = jnp.concatenate(
        [mid_back * shared_pre[:, SH_FF:] * shared_slope, mid_back * shared_act], axis=-1
    ).astype(jnp.bfloat16)
    shared_in_grad = jnp.dot(h_norm.T, shared_pre_grad, preferred_element_type=jnp.float32)
    hidden_grad = jnp.dot(shared_pre_grad, shared_in_full.T, preferred_element_type=jnp.float32)
    weight_grad = jnp.sum(cot_float[:, None, :] * expert_float, axis=-1)
    expert_cot = (
        (route_weights[:, :, None] * cot_float[:, None, :])
        .astype(jnp.bfloat16)
        .reshape(flat_count, D)
    )
    cot_ext = jnp.concatenate([expert_cot, jnp.zeros((1, D), jnp.bfloat16)], axis=0)
    send_grads = cot_ext[owner_row].reshape(experts_all, capacity, D)
    received_grad = lax.all_to_all(send_grads, "expert", split_axis=0, concat_axis=1, tiled=True)
    grads_all = lax.all_gather(received_grad, "shard", axis=1, tiled=True)
    expert_in_grad, expert_down_grad, back_part = expert_backward(
        rows_all, grads_all, gate_act, gate_slope, up_pre, expert_mid, gate_w, up_w, expert_down
    )
    back_low = lax.psum_scatter(
        back_part.astype(jnp.bfloat16), "shard", scatter_dimension=1, tiled=True
    )
    back_rows = lax.all_to_all(back_low, "expert", split_axis=1, concat_axis=0, tiled=True)
    routed_back = (
        back_rows.reshape(experts_all * capacity, D)[slot_index]
        .reshape(tok_dev, TOP, D)
        .astype(jnp.float32)
    )
    hidden_grad = hidden_grad + jnp.sum(routed_back, axis=1)
    chosen_grad = route_weights * (
        weight_grad - jnp.sum(route_weights * weight_grad, axis=-1, keepdims=True)
    )
    logit_grad = jnp.sum(route_hot * chosen_grad[:, :, None], axis=1).astype(jnp.bfloat16)
    router_grad = jnp.dot(h_norm.T, logit_grad, preferred_element_type=jnp.float32)
    hidden_grad = hidden_grad + jnp.dot(
        logit_grad, router_proj.T, preferred_element_type=jnp.float32
    )
    resid_part, ffn_gain_grad = norm_back(hidden_grad, resid, scale_ffn, gain_ffn)
    resid_grad = cot_float + resid_part
    resid_low = resid_grad.astype(jnp.bfloat16)
    out_weight_grad = jnp.dot(attended.T, resid_low, preferred_element_type=jnp.float32)
    attended_grad = (
        jnp.dot(resid_low, out_proj.T, preferred_element_type=jnp.float32)
        .astype(jnp.bfloat16)
        .reshape(tok_dev, HEADS, VDIM)
    )
    probs_full = jnp.exp(attention_scores(queries, key_nope, key_rope, allowed) - lse_rows)
    probs_again = probs_full.astype(jnp.bfloat16)
    values_grad = jnp.einsum(
        "hqk,qhd->khd", probs_again, attended_grad, preferred_element_type=jnp.float32
    )
    probs_grad = jnp.einsum(
        "qhd,khd->hqk", attended_grad, values_all, preferred_element_type=jnp.float32
    )
    delta_rows = jnp.sum(probs_full * probs_grad, axis=-1, keepdims=True)
    score_grad = (probs_full * (probs_grad - delta_rows) * score_scale).astype(jnp.bfloat16)
    query_nope_grad = jnp.einsum(
        "hqk,khd->qhd", score_grad, key_nope, preferred_element_type=jnp.float32
    )
    query_rope_grad = jnp.einsum(
        "hqk,kd->qhd", score_grad, key_rope, preferred_element_type=jnp.float32
    )
    key_nope_grad = jnp.einsum(
        "hqk,qhd->khd", score_grad, queries[..., :NOPE], preferred_element_type=jnp.float32
    )
    key_rope_grad = jnp.einsum(
        "hqk,qhd->kd", score_grad, queries[..., NOPE:], preferred_element_type=jnp.float32
    )
    key_terms = jnp.concatenate([key_nope_grad, values_grad], axis=-1).reshape(
        group_tok, HEADS * (NOPE + VDIM)
    )
    key_own, rope_own = (
        lax.psum_scatter(
            key_terms.astype(jnp.bfloat16), "shard", scatter_dimension=0, tiled=True
        ).astype(jnp.float32),
        lax.psum_scatter(
            key_rope_grad.astype(jnp.bfloat16), "shard", scatter_dimension=0, tiled=True
        ).astype(jnp.float32),
    )
    key_low = key_own.astype(jnp.bfloat16)
    kv_up_weight_grad = jnp.dot(latent[:, :KV_RANK].T, key_low, preferred_element_type=jnp.float32)
    latent_back = jnp.dot(key_low, kv_up_proj.T, preferred_element_type=jnp.float32)
    compressed_grad, kv_gain_grad = norm_back(latent_back, compressed, scale_kv, gain_kv)
    latent_grad = jnp.concatenate(
        [compressed_grad, unrotate(rope_own, cos_own, sin_own)], axis=-1
    ).astype(jnp.bfloat16)
    kv_down_weight_grad = jnp.dot(x_norm.T, latent_grad, preferred_element_type=jnp.float32)
    query_grad = (
        jnp.concatenate(
            [query_nope_grad, unrotate(query_rope_grad, cos_own[:, None, :], sin_own[:, None, :])],
            axis=-1,
        )
        .reshape(tok_dev, HEADS * (NOPE + ROPE))
        .astype(jnp.bfloat16)
    )
    query_weight_grad = jnp.dot(x_norm.T, query_grad, preferred_element_type=jnp.float32)
    norm_grad = jnp.dot(latent_grad, kv_down_proj.T, preferred_element_type=jnp.float32) + jnp.dot(
        query_grad, query_proj.T, preferred_element_type=jnp.float32
    )
    input_part, attn_gain_grad = norm_back(norm_grad, x_float, scale_in, gain_attn)
    input_grad = resid_grad + input_part
    all_sums = (
        lax.psum_scatter(attn_gain_grad, ("expert", "shard"), scatter_dimension=0, tiled=True),
        lax.psum_scatter(query_weight_grad, ("expert", "shard"), scatter_dimension=0, tiled=True),
        lax.psum_scatter(kv_down_weight_grad, ("expert", "shard"), scatter_dimension=0, tiled=True),
        lax.psum_scatter(kv_gain_grad, ("expert", "shard"), scatter_dimension=0, tiled=True),
        lax.psum_scatter(kv_up_weight_grad, ("expert", "shard"), scatter_dimension=0, tiled=True),
        lax.psum_scatter(out_weight_grad, ("expert", "shard"), scatter_dimension=0, tiled=True),
        lax.psum_scatter(ffn_gain_grad, ("expert", "shard"), scatter_dimension=0, tiled=True),
        lax.psum_scatter(router_grad, ("expert", "shard"), scatter_dimension=0, tiled=True),
        lax.psum_scatter(shared_in_grad, ("expert", "shard"), scatter_dimension=0, tiled=True),
        lax.psum_scatter(shared_down_grad, ("expert", "shard"), scatter_dimension=0, tiled=True),
    )
    return (
        block_out,
        input_grad,
        all_sums[0],
        all_sums[1],
        all_sums[2],
        all_sums[3],
        all_sums[4],
        all_sums[5],
        all_sums[6],
        all_sums[7],
        all_sums[8],
        all_sums[9],
        expert_in_grad,
        expert_down_grad,
    )


def solution(mesh):
    in_specs = (
        P(("expert", "shard"), None),
        P(("expert", "shard"), None),
        P("expert", None),
        P(("expert", "shard"), None),
        P("shard"),
        P("shard", None),
        P("shard", None),
        P("shard"),
        P("shard", None),
        P("shard", None),
        P("shard"),
        P("shard", None),
        P("shard", None),
        P("shard", None),
        P("expert", None, "shard"),
        P("expert", None, "shard"),
    )
    out_specs = (
        P(("expert", "shard"), None),
        P(("expert", "shard"), None),
        P(("expert", "shard")),
        P(("expert", "shard"), None),
        P(("expert", "shard"), None),
        P(("expert", "shard")),
        P(("expert", "shard"), None),
        P(("expert", "shard"), None),
        P(("expert", "shard")),
        P(("expert", "shard"), None),
        P(("expert", "shard"), None),
        P(("expert", "shard"), None),
        P("expert", None, "shard"),
        P("expert", None, "shard"),
    )
    return jax.shard_map(local, mesh=mesh, in_specs=in_specs, out_specs=out_specs, check_vma=False)
```

profile of v0, /device:TPU:0, one launch (start us, length us, event | category | flops | bytes accessed | tf_op | source)
XLA Modules:
  0.0 5149.6 jit_solution(8924839339749894789)
XLA Ops:
  67.8 21.8 all_gather.42
  89.6 60.9 %all-gather.14.cloned.1.call-done = bf16[512,4096]{1,0:T(8,128)(2,1)} async-done(((bf16[128,4096]{1,0:T(8,128)(2,1)}), bf16[512,4096]{1,0:T(8,128)(2,1)}) %all-gather.14.cloned.1.call-update) | async-done | bytes 4194320 | tf_op jit(solution)/shard_map/all_gather | solution.py:164
  164.1 204.4 %all-gather.16.cloned.1.call-done = bf16[2048,3072]{1,0:T(8,128)(2,1)} async-done(((bf16[512,3072]{1,0:T(8,128)(2,1)}), bf16[2048,3072]{1,0:T(8,128)(2,1)}) %all-gather.16.cloned.1.call-update) | async-done | bytes 12582928 | tf_op jit(solution)/shard_map/all_gather | solution.py:161
  385.0 132.7 %all-gather.18.cloned.1.call-done = bf16[2048,2048]{1,0:T(8,128)(2,1)} async-done(((bf16[512,2048]{1,0:T(8,128)(2,1)}), bf16[2048,2048]{1,0:T(8,128)(2,1)}) %all-gather.18.cloned.1.call-update) | async-done | bytes 8388624 | tf_op jit(solution)/shard_map/all_gather | solution.py:165
  530.6 52.7 %all_to_all.66 = bf16[16,64,2048]{2,1,0:T(8,128)(2,1)S(1)} all-to-all(bf16[16,64,2048]{2,1,0:T(8,128)(2,1)} %bitcast.136), channel_id=1, replica_groups=mesh['expert'=8,'shard'=4] {'expert'}, dimensions={0} | all-to-all | bytes 8388608 | tf_op jit(solution)/shard_map/all_to_all | solution.py:241
  600.9 23.4 all_gather.49
  642.9 52.7 %all_to_all.67 = bf16[16,64,2048]{2,1,0:T(8,128)(2,1)S(1)} all-to-all(bf16[16,64,2048]{2,1,0:T(8,128)(2,1)} %bitcast.137), channel_id=1, replica_groups=mesh['expert'=8,'shard'=4] {'expert'}, dimensions={0} | all-to-all | bytes 8388608 | tf_op jit(solution)/shard_map/all_to_all | solution.py:272
  697.9 172.1 %all-gather.24.cloned.1.call-done = bf16[2,2048,2048]{2,1,0:T(8,128)(2,1)} async-done(((bf16[2,512,2048]{2,1,0:T(8,128)(2,1)}), bf16[2,2048,2048]{2,1,0:T(8,128)(2,1)}) %all-gather.24.cloned.1.call-update) | async-done | bytes 16777232 | tf_op jit(solution)/shard_map/all_gather | solution.py:242
  895.4 261.1 %all-gather.26.cloned.1.call-done = bf16[2,2048,2048]{2,1,0:T(8,128)(2,1)} async-done(((bf16[2,512,2048]{2,1,0:T(8,128)(2,1)}), bf16[2,2048,2048]{2,1,0:T(8,128)(2,1)}) %all-gather.26.cloned.1.call-update) | async-done | bytes 16777232 | tf_op jit(solution)/shard_map/all_gather | solution.py:273
  1156.5 15.3 multiply_convert_fusion.1
  1171.8 14.6 convolution_convert_fusion
  1188.2 17.4 fusion.11
  1205.6 20.0 add_convert_fusion
  1226.9 238.2 %reduce-scatter.18.cloned.1.call-done = bf16[2,512,2048]{2,1,0:T(8,128)(2,1)} async-done(((bf16[2,2048,2048]{2,1,0:T(8,128)(2,1)}), bf16[2,512,2048]{2,1,0:T(8,128)(2,1)}) %reduce-scatter.18.cloned.1.call-update) | async-done | bytes 4194320 | tf_op jit(solution)/shard_map/reduce_scatter | solution.py:248
  1478.4 270.2 %reduce-scatter.20.cloned.1.call-done = bf16[2,512,2048]{2,1,0:T(8,128)(2,1)} async-done(((bf16[2,2048,2048]{2,1,0:T(8,128)(2,1)}), bf16[2,512,2048]{2,1,0:T(8,128)(2,1)}) %reduce-scatter.20.cloned.1.call-update) | async-done | bytes 4194320 | tf_op jit(solution)/shard_map/reduce_scatter | solution.py:277
  1762.2 379.8 %all-gather.20.cloned.1.call-done = bf16[2048,5632]{1,0:T(8,128)(2,1)} async-done(((bf16[512,5632]{1,0:T(8,128)(2,1)}), bf16[2048,5632]{1,0:T(8,128)(2,1)}) %all-gather.20.cloned.1.call-update) | async-done | bytes 23068688 | tf_op jit(solution)/shard_map/all_gather | solution.py:168
  2155.1 187.8 %all-gather.22.cloned.1.call-done = bf16[2816,2048]{1,0:T(8,128)(2,1)} async-done(((bf16[704,2048]{1,0:T(8,128)(2,1)}), bf16[2816,2048]{1,0:T(8,128)(2,1)}) %all-gather.22.cloned.1.call-update) | async-done | bytes 11534352 | tf_op jit(solution)/shard_map/all_gather | solution.py:169
  2443.6 19.7 convert_bitcast_fusion.1
  2463.4 17.2 fusion.51
  2506.0 70.0 %reduce-scatter.34.cloned.1.call-done = bf16[128,4096]{1,0:T(8,128)(2,1)} async-done(((bf16[512,4096]{1,0:T(8,128)(2,1)}), bf16[128,4096]{1,0:T(8,128)(2,1)}) %reduce-scatter.34.cloned.1.call-update) | async-done | bytes 1048592
  2601.0 17.4 fusion.40
  2619.1 19.6 fusion.43
  2650.8 19.4 fusion.63
  2670.2 14.3 fusion.116
  2707.0 14.3 fusion.118
  2744.5 43.8 all-reduce.5
  2793.6 416.0 %reduce-scatter.32.cloned.1.call-done = f32[88,2048]{1,0:T(8,128)} async-done(((f32[2816,2048]{1,0:T(8,128)}), f32[88,2048]{1,0:T(8,128)}) %reduce-scatter.32.cloned.1.call-update) | async-done | bytes 720912 | tf_op jit(solution)/shard_map/reduce_scatter | solution.py:369
  3209.6 155.1 %reduce-scatter.24.cloned.1.call-done = f32[64,576]{1,0:T(8,128)} async-done(((f32[2048,576]{1,0:T(8,128)}), f32[64,576]{1,0:T(8,128)}) %reduce-scatter.24.cloned.1.call-update) | async-done | bytes 147472 | tf_op jit(solution)/shard_map/reduce_scatter | solution.py:362
  3364.7 187.2 %reduce-scatter.26.cloned.1.call-done = f32[16,4096]{1,0:T(8,128)} async-done(((f32[512,4096]{1,0:T(8,128)}), f32[16,4096]{1,0:T(8,128)}) %reduce-scatter.26.cloned.1.call-update) | async-done | bytes 262160 | tf_op jit(solution)/shard_map/reduce_scatter | solution.py:364
  3551.8 364.7 %reduce-scatter.28.cloned.1.call-done = f32[64,2048]{1,0:T(8,128)} async-done(((f32[2048,2048]{1,0:T(8,128)}), f32[64,2048]{1,0:T(8,128)}) %reduce-scatter.28.cloned.1.call-update) | async-done | bytes 524304 | tf_op jit(solution)/shard_map/reduce_scatter | solution.py:365
  3916.6 251.4 %reduce-scatter.22.cloned.1.call-done = f32[64,3072]{1,0:T(8,128)} async-done(((f32[2048,3072]{1,0:T(8,128)}), f32[64,3072]{1,0:T(8,128)}) %reduce-scatter.22.cloned.1.call-update) | async-done | bytes 786448 | tf_op jit(solution)/shard_map/reduce_scatter | solution.py:361
  4168.0 974.9 %reduce-scatter.30.cloned.1.call-done = f32[64,5632]{1,0:T(8,128)} async-done(((f32[2048,5632]{1,0:T(8,128)}), f32[64,5632]{1,0:T(8,128)}) %reduce-scatter.30.cloned.1.call-update) | async-done | bytes 1441808 | tf_op jit(solution)/shard_map/reduce_scatter | solution.py:368
  (325 shorter events, 424.5 us)
Async XLA Ops:
  7.2 1149.3 %copy-start = (bf16[2,2048,352]{1,2,0:T(8,128)(2,1)S(1)}, bf16[2,2048,352]{1,2,0:T(8,128)(2,1)}, u32[]{:S(2)}) copy-start(bf16[2,2048,352]{1,2,0:T(8,128)(2,1)} %param.31) | copy-start | bytes 8650756
  7.3 55.7 %all-gather.12.cloned.1.call-start = ((), (), s32[]{:S(2)}) async-start(), calls=%async_computation.15 | async-start | bytes 2949120 | tf_op jit(solution)/shard_map/all_gather | solution.py:162
  8.0 142.4 %all-gather.14.cloned.1.call-start = ((), (), s32[]{:S(2)}) async-start(), calls=%async_computation.16 | async-start | bytes 5242880 | tf_op jit(solution)/shard_map/all_gather | solution.py:164
  8.7 359.7 %all-gather.16.cloned.1.call-start = ((), (), s32[]{:S(2)}) async-start(), calls=%async_computation.17 | async-start | bytes 15728640 | tf_op jit(solution)/shard_map/all_gather | solution.py:161
  9.5 508.2 %all-gather.18.cloned.1.call-start = ((), (), s32[]{:S(2)}) async-start(), calls=%async_computation.18 | async-start | bytes 10485760 | tf_op jit(solution)/shard_map/all_gather | solution.py:165
  10.1 860.0 %all-gather.24.cloned.1.call-start = ((), (), s32[]{:S(2)}) async-start(), calls=%async_computation.21 | async-start | bytes 20971520 | tf_op jit(solution)/shard_map/all_gather | solution.py:242
  24.8 343.7 %copy-start.26 = (f32[4,1,512]{2,1,0:T(1,128)}, f32[4,1,512]{2,1,0:T(1,128)S(1)}, u32[]{:S(2)}) copy-start(f32[4,1,512]{2,1,0:T(1,128)S(1)} %convert_element_type.154) | copy-start | bytes 24580
  35.7 119.5 %copy-start.53 = (f32[4,1,128]{2,1,0:T(1,128)}, f32[4,1,128]{2,1,0:T(1,128)S(1)}, u32[]{:S(2)}) copy-start(f32[4,1,128]{2,1,0:T(1,128)S(1)} %convert_element_type.155) | copy-start | bytes 6148
  47.9 475.4 %copy-start.42 = (f32[4,1,512]{2,1,0:T(1,128)}, f32[4,1,512]{2,1,0:T(1,128)S(1)}, u32[]{:S(2)}) copy-start(f32[4,1,512]{2,1,0:T(1,128)S(1)} %convert_element_type.156) | copy-start | bytes 24580
  59.2 309.3 %copy-start.51 = (f32[128]{0:T(128)}, f32[128]{0:T(128)S(1)}, u32[]{:S(2)}) copy-start(f32[128]{0:T(128)S(1)} %get-tuple-element.45) | copy-start | bytes 1540
  66.9 309.8 %copy-start.36 = (f32[128,32]{0,1:T(8,128)}, f32[128,32]{0,1:T(8,128)S(1)}, u32[]{:S(2)}) copy-start(f32[128,32]{0,1:T(8,128)S(1)} %get-tuple-element.26) | copy-start | bytes 49156
  66.9 309.8 %copy-start.38 = (f32[128,32]{0,1:T(8,128)}, f32[128,32]{0,1:T(8,128)S(1)}, u32[]{:S(2)}) copy-start(f32[128,32]{0,1:T(8,128)S(1)} %get-tuple-element.27) | copy-start | bytes 49156
  383.2 139.4 %copy-start.44 = (f32[16,128]{1,0:T(8,128)}, f32[16,128]{1,0:T(8,128)S(1)}, u32[]{:S(2)}) copy-start(f32[16,128]{1,0:T(8,128)S(1)} %log_add_fusion) | copy-start | bytes 24580
  585.7 570.8 %all-gather.26.cloned.1.call-start = ((), (), s32[]{:S(2)}) async-start(), calls=%async_computation.23 | async-start | bytes 20971520 | tf_op jit(solution)/shard_map/all_gather | solution.py:273
  697.9 767.2 %reduce-scatter.18.cloned.1.call-start = ((), (), s32[]{:S(2)}) async-start(), calls=%async_computation.22 | async-start | bytes 20971520 | tf_op jit(solution)/shard_map/reduce_scatter | solution.py:248
  1186.4 562.2 %reduce-scatter.20.cloned.1.call-start = ((), (), s32[]{:S(2)}) async-start(), calls=%async_computation.24 | async-start | bytes 20971520 | tf_op jit(solution)/shard_map/reduce_scatter | solution.py:277
  1225.6 916.5 %all-gather.20.cloned.1.call-start = ((), (), s32[]{:S(2)}) async-start(), calls=%async_computation.19 | async-start | bytes 28835840 | tf_op jit(solution)/shard_map/all_gather | solution.py:168
  1226.3 1116.5 %all-gather.22.cloned.1.call-start = ((), (), s32[]{:S(2)}) async-start(), calls=%async_computation.20 | async-start | bytes 14417920 | tf_op jit(solution)/shard_map/all_gather | solution.py:169
  1473.6 283.6 %all-to-all-start.1 = ((bf16[2,512,2048]{2,0,1:T(2,128)(2,1)}), bf16[2,512,2048]{2,0,1:T(2,128)(2,1)}, u32[]{:S(2)}, u32[]{:S(2)}) async-start(bf16[2,512,2048]{2,0,1:T(2,128)(2,1)} %copy.154), calls=%async_computation.2 | async-start | bytes 8388608 | tf_op jit(solution)/shard_map/all_to_all | solution.py:251
  1757.2 384.9 %copy-start.10 = (bf16[128,2048]{1,0:T(8,128)(2,1)S(1)}, bf16[128,2048]{1,0:T(8,128)(2,1)}, u32[]{:S(2)}) copy-start(bf16[128,2048]{1,0:T(8,128)(2,1)} %copy-done.8) | copy-start | bytes 1572868
  1757.2 626.6 %all-to-all-start.3 = ((bf16[2,512,2048]{2,0,1:T(2,128)(2,1)}), bf16[2,512,2048]{2,0,1:T(2,128)(2,1)}, u32[]{:S(2)}, u32[]{:S(2)}) async-start(bf16[2,512,2048]{2,0,1:T(2,128)(2,1)} %copy.158), calls=%async_computation.5 | async-start | bytes 8388608 | tf_op jit(solution)/shard_map/all_to_all | solution.py:280
  1762.0 742.8 %reduce-scatter.36.cloned.1.call-start = ((), (), s32[]{:S(2)}) async-start(), calls=%async_computation.32 | async-start | bytes 163840
  2427.3 164.4 %copy-start.12 = (f32[128,2048]{1,0:T(8,128)}, f32[128,2048]{1,0:T(8,128)S(1)}, u32[]{:S(2)}) copy-start(f32[128,2048]{1,0:T(8,128)S(1)} %subtract_add_fusion) | copy-start | bytes 3145732
  2481.3 94.7 %reduce-scatter.34.cloned.1.call-start = ((), (), s32[]{:S(2)}) async-start(), calls=%async_computation.31 | async-start | bytes 5242880
  2492.6 245.9 %reduce-scatter.38.cloned.1.call-start = ((), (), s32[]{:S(2)}) async-start(), calls=%async_computation.33 | async-start | bytes 1081344
  2494.1 715.5 %reduce-scatter.32.cloned.1.call-start = ((), (), s32[]{:S(2)}) async-start(), calls=%async_computation.30 | async-start | bytes 23789568 | tf_op jit(solution)/shard_map/reduce_scatter | solution.py:369
  2504.7 859.9 %reduce-scatter.24.cloned.1.call-start = ((), (), s32[]{:S(2)}) async-start(), calls=%async_computation.26 | async-start | bytes 5406720 | tf_op jit(solution)/shard_map/reduce_scatter | solution.py:362
  2584.9 966.9 %reduce-scatter.26.cloned.1.call-start = ((), (), s32[]{:S(2)}) async-start(), calls=%async_computation.27 | async-start | bytes 8650752 | tf_op jit(solution)/shard_map/reduce_scatter | solution.py:364
  2591.6 1325.0 %reduce-scatter.28.cloned.1.call-start = ((), (), s32[]{:S(2)}) async-start(), calls=%async_computation.28 | async-start | bytes 17301504 | tf_op jit(solution)/shard_map/reduce_scatter | solution.py:365
  2600.9 1567.1 %reduce-scatter.22.cloned.1.call-start = ((), (), s32[]{:S(2)}) async-start(), calls=%async_computation.25 | async-start | bytes 25952256 | tf_op jit(solution)/shard_map/reduce_scatter | solution.py:361
  2650.7 2492.1 %reduce-scatter.30.cloned.1.call-start = ((), (), s32[]{:S(2)}) async-start(), calls=%async_computation.29 | async-start | bytes 47579136 | tf_op jit(solution)/shard_map/reduce_scatter | solution.py:368
  2738.6 2404.3 %copy-start.1 = (bf16[2,2048,352]{1,2,0:T(8,128)(2,1)S(1)}, bf16[2,2048,352]{1,2,0:T(8,128)(2,1)}, u32[]{:S(2)}) copy-start(bf16[2,2048,352]{1,2,0:T(8,128)(2,1)} %param.31) | copy-start | bytes 8650756
  (64 other events, 1098.5 us)
Sparse Core Ops, SparseCore 0:
  9.7 53.2 all-gather.11
  64.5 85.8 all-gather.13
  152.0 216.3 all-gather.15
  369.9 147.8 all-gather.17
  585.8 284.1 all-gather.23
  871.5 285.0 all-gather.25
  1186.6 278.4 reduce-scatter.17
  1467.6 281.0 reduce-scatter.19
  1750.2 391.7 all-gather.19
  2143.5 199.3 all-gather.21
  2481.4 17.3 reduce-scatter.35
  2501.1 74.8 reduce-scatter.33
  2578.3 136.2 reduce-scatter.37
  2717.4 492.1 reduce-scatter.31
  3212.4 152.2 reduce-scatter.23
  3367.5 184.3 reduce-scatter.25
  3554.7 361.8 reduce-scatter.27
  3924.5 243.3 reduce-scatter.21
  4170.8 971.9 reduce-scatter.29
where the time goes:
time: 5160 us; the launch traced here: 5150 us
  waiting for transfers between devices  4330 us (84%)
  matrix products  371 us (7%)
  blocking collectives  230 us (4%)
  local copies, waits for them, and re-layouts  140 us (3%)
    reduce_scatter x1, waiting for transfers between devices, local(): lax.psum_scatter(shared_in_grad, ('expert', 'shard'), scatter_dimension=0...  975 us
    reduce_scatter x1, waiting for transfers between devices, local(): lax.psum_scatter(shared_down_grad, ('expert', 'shard'), scatter_dimension...  416 us
    all_gather x1, waiting for transfers between devices, local(): lax.all_gather(shared_in, 'shard', axis=0, tiled=True)  380 us
    reduce_scatter x1, waiting for transfers between devices, local(): lax.psum_scatter(out_weight_grad, ('expert', 'shard'), scatter_dimension=...  365 us
    reduce_scatter x1, waiting for transfers between devices, local(): lax.psum_scatter(back_part.astype(jnp.bfloat16), 'shard', scatter_dimensi...  270 us
    all_gather x1, waiting for transfers between devices, local(): grads_all = lax.all_gather(received_grad, 'shard', axis=1, tiled=True)  261 us
    reduce_scatter x1, waiting for transfers between devices, local(): lax.psum_scatter(query_weight_grad, ('expert', 'shard'), scatter_dimensio...  251 us
    reduce_scatter x1, waiting for transfers between devices, local(): lax.psum_scatter(partial_value.astype(jnp.bfloat16), 'shard', scatter_dim...  238 us
  transfers between devices with their start and end apart: 21, of which 17 were waited for; matrix products, arithmetic and copies ran while one was open for 8% of the time, Pallas kernels for 0%

commit v1 on v0

v1 whole, which is shorter than its diff:
```python
import jax
import jax.numpy as jnp
from jax import lax
from jax.sharding import PartitionSpec as P

D = 2048
HEADS = 16
NOPE = 128
ROPE = 64
VDIM = 128
QK = NOPE + ROPE
KV_RANK = 512
SH_FF = 2816
EXP_DEV = 2
FF_PAD = 896

EPS = 1e-06
ROPE_BASE = 10000.0
BOTH = ("expert", "shard")
bf16 = jnp.bfloat16
f32 = jnp.float32


def dot(a, b, dims):
    return lax.dot_general(a, b, (dims, ((), ())), preferred_element_type=f32)


def mm(a, b):
    return dot(a, b, ((1,), (0,)))


def mm_tn(a, b):
    return dot(a, b, ((0,), (0,)))


def mm_nt(a, b):
    return dot(a, b, ((1,), (1,)))


def inv_rms(values):
    return lax.rsqrt(jnp.mean(values * values, axis=-1, keepdims=True) + EPS)


def norm_back(grad_out, values, inv_scale, gain_row):
    scaled = grad_out * gain_row
    grad_in = inv_scale * scaled - values * inv_scale**3 * jnp.mean(
        scaled * values, axis=-1, keepdims=True
    )
    grad_gain = jnp.sum(grad_out * values * inv_scale, axis=0)
    return (grad_in, grad_gain)


def rope_tables(doc_row):
    count = doc_row.shape[0]
    index = jnp.arange(count, dtype=jnp.int32)
    before = (doc_row[:, None] == doc_row[None, :]) & (index[None, :] < index[:, None])
    positions = jnp.sum(before.astype(f32), axis=1)
    half = ROPE // 2
    frequency = ROPE_BASE ** (-jnp.arange(half, dtype=f32) / half)
    angles = positions[:, None] * frequency[None, :]
    return (jnp.cos(angles), jnp.sin(angles))


def rotate(values, cosine, sine):
    half = cosine.shape[-1]
    a, b = values[..., :half], values[..., half:]
    return jnp.concatenate([a * cosine - b * sine, b * cosine + a * sine], axis=-1)


def unrotate(values, cosine, sine):
    return rotate(values, cosine, -sine)


def swap(value, bit, count):
    return lax.ppermute(value, "expert", [(i, i ^ bit) for i in range(count)])


def plane_gather(v, count):
    if count != 8:
        return lax.all_gather(v, "expert", axis=0)
    half = v.shape[-1] // 2
    vx, vy = swap(v, 2, count), swap(v, 4, count)
    vd = jnp.concatenate(
        [swap(vx[..., :half], 4, count), swap(vy[..., half:], 2, count)], axis=-1
    )
    parts = []
    for part in (v, vx, vy, vd):
        parts += [part, swap(part, 1, count)]
    return jnp.stack(parts)


def plane_reduce(p, count):
    if count != 8:
        return lax.psum_scatter(p, "expert", scatter_dimension=0, tiled=False)
    kind = p.dtype
    half = p.shape[-1] // 2
    r = [p[j].astype(f32) + swap(p[j + 1], 1, count).astype(f32) for j in (0, 2, 4, 6)]
    low = r[3].astype(kind)
    r1a = r[1][..., half:] + swap(low[..., half:], 4, count).astype(f32)
    r2a = r[2][..., :half] + swap(low[..., :half], 2, count).astype(f32)
    r1 = jnp.concatenate([r[1][..., :half], r1a], axis=-1).astype(kind)
    r2 = jnp.concatenate([r2a, r[2][..., half:]], axis=-1).astype(kind)
    return r[0] + swap(r1, 2, count).astype(f32) + swap(r2, 4, count).astype(f32)


def local(
    block_in,
    cotangent,
    doc_ids,
    routes,
    attn_gain,
    query_weight,
    kv_down_weight,
    kv_gain,
    kv_up_weight,
    out_weight,
    ffn_gain,
    router_weight,
    shared_in,
    shared_down,
    expert_in,
    expert_down,
):
    tok = block_in.shape[0]
    E, S = lax.axis_size("expert"), lax.axis_size("shard")
    e, s = lax.axis_index("expert"), lax.axis_index("shard")
    group = tok * S
    heads = HEADS // S
    units = SH_FF // (E * S)
    experts_all = EXP_DEV * E
    ff = expert_in.shape[2]
    first = s * tok
    scale = QK ** (-0.5)

    def own(v):
        return lax.dynamic_slice_in_dim(v, first, tok, 0)

    def gather(v):
        return lax.all_gather(v, "shard", axis=0, tiled=True)

    gain_a, gain_f, gain_k = gather(attn_gain), gather(ffn_gain), gather(kv_gain)
    router = gather(router_weight)
    kv_down = gather(kv_down_weight)
    w_out = gather(out_weight)

    def columns_to_heads(w):
        rows, cols = w.shape
        parts = w.reshape(rows, S, cols // S)
        return lax.all_to_all(parts, "shard", split_axis=1, concat_axis=0, tiled=True).reshape(
            rows * S, cols // S
        )

    w_q = columns_to_heads(query_weight)
    kv_up = columns_to_heads(kv_up_weight)
    x_rows = gather(block_in)
    cot_rows = gather(cotangent)
    routes_rows = gather(routes)

    def shared_columns(w, start):
        part = lax.dynamic_slice_in_dim(w, start + e * S * units, S * units, 1)
        return columns_to_heads(part)

    sh_gate, sh_up = shared_columns(shared_in, 0), shared_columns(shared_in, SH_FF)
    rows_here = shared_down.shape[0]
    sends = []
    for j in range(S):
        at = (e * S + j) * units - s * rows_here
        sends.append(lax.dynamic_slice_in_dim(shared_down, jnp.clip(at, 0, rows_here - units), units, 0))
    got = lax.all_to_all(jnp.stack(sends), "shard", split_axis=0, concat_axis=0, tiled=True)
    sh_down = lax.dynamic_index_in_dim(got, (e * S + s) * units // rows_here, 0, keepdims=False)

    pad = jnp.zeros((D, FF_PAD - EXP_DEV * ff - units), bf16)
    w_in = jnp.concatenate(
        [expert_in[0, :D], expert_in[1, :D], sh_gate, pad, expert_in[0, D:], expert_in[1, D:], sh_up, pad],
        axis=1,
    )
    w_down = jnp.concatenate([expert_down[0], expert_down[1], sh_down.T, pad], axis=1)

    doc_row = doc_ids[0]
    cosine, sine = rope_tables(doc_row)
    index = jnp.arange(group, dtype=jnp.int32)
    allowed = (doc_row[:, None] == doc_row[None, :]) & (index[None, :] <= index[:, None])
    x_float = x_rows.astype(f32)
    scale_in = inv_rms(x_float)
    x_norm = (x_float * scale_in * gain_a).astype(bf16)
    query_raw = mm(x_norm, w_q).reshape(group, heads, QK)
    queries = jnp.concatenate(
        [
            query_raw[..., :NOPE],
            rotate(query_raw[..., NOPE:], cosine[:, None, :], sine[:, None, :]),
        ],
        axis=-1,
    ).astype(bf16)
    latent_raw = mm(x_norm, kv_down)
    compressed = latent_raw[:, :KV_RANK]
    scale_kv = inv_rms(compressed)
    latent = (compressed * scale_kv * gain_k).astype(bf16)
    key_rope = rotate(latent_raw[:, KV_RANK:], cosine, sine).astype(bf16)
    expanded = mm(latent, kv_up).astype(bf16).reshape(group, heads, NOPE + VDIM)
    keys = jnp.concatenate(
        [expanded[..., :NOPE], jnp.broadcast_to(key_rope[:, None, :], (group, heads, ROPE))], axis=-1
    )
    values = expanded[..., NOPE:]
    scores = jnp.einsum("qhd,khd->hqk", queries, keys, preferred_element_type=f32)
    scores = jnp.where(allowed[None], scores * scale, -jnp.inf)
    row_max = jnp.max(scores, axis=-1, keepdims=True)
    lse = row_max + jnp.log(jnp.sum(jnp.exp(scores - row_max), axis=-1, keepdims=True))
    probs = jnp.exp(scores - lse)
    probs_low = probs.astype(bf16)
    attended = (
        jnp.einsum("hqk,khd->qhd", probs_low, values, preferred_element_type=f32)
        .astype(bf16)
        .reshape(group, heads * VDIM)
    )
    attended_all = lax.all_gather(attended, "shard", axis=1, tiled=True)

    resid = x_float + mm(attended_all, w_out)
    scale_ffn = inv_rms(resid)
    h_norm = (resid * scale_ffn * gain_f).astype(bf16)
    logits = mm(h_norm, router)
    expert_ids = jnp.arange(experts_all, dtype=jnp.int32)
    named = jnp.any(routes_rows[:, :, None] == expert_ids[None, None, :], axis=1)
    masked = jnp.where(named, logits, -jnp.inf)
    top = jnp.exp(masked - jnp.max(masked, axis=-1, keepdims=True))
    route_w = top / jnp.sum(top, axis=-1, keepdims=True)

    unit_at = slice(EXP_DEV * ff, EXP_DEV * ff + units)
    spot = (expert_ids[:, None] == (e * EXP_DEV + jnp.arange(EXP_DEV, dtype=jnp.int32))[None, :]).astype(f32)

    def hidden_units(h_rows, cot_part, w_rows):
        part = h_rows.shape[0]
        count = E * part
        h_all = plane_gather(h_rows, E).reshape(count, D)
        cot_all = plane_gather(cot_part, E).reshape(count, D)
        w_own = lax.dynamic_slice_in_dim(plane_gather(w_rows.T, E), e * EXP_DEV, EXP_DEV, 1)
        cols = w_own.transpose(0, 2, 1).reshape(count, EXP_DEV)
        weight = jnp.concatenate(
            [
                jnp.broadcast_to(cols[:, :1], (count, ff)),
                jnp.broadcast_to(cols[:, 1:], (count, ff)),
                jnp.ones((count, FF_PAD - EXP_DEV * ff), f32),
            ],
            axis=1,
        )
        pre = mm(h_all, w_in)
        gate_pre, up_pre = pre[:, :FF_PAD], pre[:, FF_PAD:]
        mid_grad = mm(cot_all, w_down)
        sigmoid = jax.nn.sigmoid(gate_pre)
        act = gate_pre * sigmoid
        slope = sigmoid * (1.0 + gate_pre * (1.0 - sigmoid))
        mid = act * up_pre
        mid_low = (weight * mid).astype(bf16)
        weighted = weight * mid_grad
        gate_grad = (weighted * up_pre * slope).astype(bf16)
        up_grad = (weighted * act).astype(bf16)
        product = mid * mid_grad
        wg = jnp.stack([jnp.sum(product[:, k * ff : (k + 1) * ff], axis=1) for k in range(EXP_DEV)])
        out_part = mm_nt(mid_low, w_down).astype(bf16).reshape(E, part, D)
        pre_grad = jnp.concatenate([gate_grad, up_grad], axis=1)
        back_part = mm_nt(pre_grad, w_in).astype(bf16).reshape(E, part, D)
        in_grad = jnp.stack(
            [
                jnp.concatenate([mm_tn(h_all, g[:, k * ff : (k + 1) * ff]) for g in (gate_grad, up_grad)], axis=0)
                for k in range(EXP_DEV)
            ]
        )
        down_grad = jnp.stack([mm_tn(cot_all, mid_low[:, k * ff : (k + 1) * ff]) for k in range(EXP_DEV)])
        sh_down_grad = mm_tn(mid_low[:, unit_at], cot_all)
        sh_in_grad = mm_tn(h_all, jnp.concatenate([gate_grad[:, unit_at], up_grad[:, unit_at]], axis=1))
        wg = wg.reshape(EXP_DEV, E, part).transpose(1, 0, 2)
        wg_full = jnp.sum(spot[None, :, :, None] * wg[:, None, :, :], axis=2)
        sums = (plane_reduce(out_part, E), plane_reduce(back_part, E), plane_reduce(wg_full, E).T)
        return ((in_grad, down_grad, sh_down_grad, sh_in_grad), sums)

    pieces = max(1, E // 8)
    if pieces == 1:
        grads, sums = hidden_units(h_norm, cot_rows, route_w)
    else:
        rows_in = [v.reshape(pieces, -1, v.shape[-1]) for v in (h_norm, cot_rows, route_w)]

        def one(total, rows):
            made, sums = hidden_units(*rows)
            return (jax.tree.map(jnp.add, total, made), sums)

        zeros = (
            jnp.zeros(expert_in.shape, f32),
            jnp.zeros(expert_down.shape, f32),
            jnp.zeros((units, D), f32),
            jnp.zeros((D, 2 * units), f32),
        )
        grads, sums = lax.scan(one, zeros, tuple(rows_in))
        sums = [v.reshape(-1, v.shape[-1]) for v in sums]
    expert_in_grad, expert_down_grad, shared_down_grad, sh_in_grad = grads
    sh_in_grad = lax.all_to_all(
        sh_in_grad.reshape(E * S, D // (E * S), 2 * units), BOTH, split_axis=0, concat_axis=0, tiled=True
    )
    shared_in_grad = (
        sh_in_grad.reshape(E * S, D // (E * S), 2, units).transpose(1, 2, 0, 3).reshape(D // (E * S), 2 * SH_FF)
    )
    out_sum, back_sum, wg_sum = sums

    def owners_sum(part):
        return lax.psum_scatter(part, "shard", scatter_dimension=0, tiled=True).astype(f32)

    routed = owners_sum(out_sum.astype(bf16))
    hidden_grad = owners_sum(back_sum.astype(bf16))
    weight_grad = owners_sum(wg_sum)

    resid_own, h_own, w_tok, scale_own = own(resid), own(h_norm), own(route_w), own(scale_ffn)
    block_out = resid_own + routed
    logit_grad = (w_tok * (weight_grad - jnp.sum(w_tok * weight_grad, axis=-1, keepdims=True))).astype(bf16)
    router_grad = mm_tn(h_own, logit_grad)
    hidden_grad = hidden_grad + mm_nt(logit_grad, router)
    resid_part, ffn_gain_grad = norm_back(hidden_grad, resid_own, scale_own, gain_f)
    resid_grad = cotangent.astype(f32) + resid_part
    resid_low = resid_grad.astype(bf16)

    attended_grad = mm_nt(resid_low, w_out).astype(bf16)
    both = jnp.concatenate([attended_grad, resid_low], axis=1).reshape(tok, 2, S, D // S)
    both = lax.all_to_all(both, "shard", split_axis=2, concat_axis=0, tiled=True).reshape(group, 2, D // S)
    att_grad = both[:, 0].reshape(group, heads, VDIM)
    resid_cols = both[:, 1]
    out_grad = mm_tn(attended_all, resid_cols)

    values_grad = jnp.einsum("hqk,qhd->khd", probs_low, att_grad, preferred_element_type=f32)
    probs_grad = jnp.einsum("qhd,khd->hqk", att_grad, values, preferred_element_type=f32)
    delta = jnp.sum(probs * probs_grad, axis=-1, keepdims=True)
    score_grad = (probs * (probs_grad - delta) * scale).astype(bf16)
    q_grad = jnp.einsum("hqk,khd->qhd", score_grad, keys, preferred_element_type=f32)
    k_grad = jnp.einsum("hqk,qhd->khd", score_grad, queries, preferred_element_type=f32)
    rope_part = jnp.sum(k_grad[..., NOPE:], axis=1)
    key_grad = (
        jnp.concatenate([k_grad[..., :NOPE], values_grad], axis=-1)
        .reshape(group, heads * (NOPE + VDIM))
        .astype(bf16)
    )
    query_grad = (
        jnp.concatenate(
            [q_grad[..., :NOPE], unrotate(q_grad[..., NOPE:], cosine[:, None, :], sine[:, None, :])], axis=-1
        )
        .reshape(group, heads * QK)
        .astype(bf16)
    )
    latent_part = jnp.concatenate([mm_nt(key_grad, kv_up), rope_part], axis=1)
    norm_part = mm_nt(query_grad, w_q)
    latent_back = lax.psum_scatter(latent_part.astype(bf16), "shard", scatter_dimension=0, tiled=True).astype(f32)
    norm_sum = lax.psum_scatter(norm_part.astype(bf16), "shard", scatter_dimension=0, tiled=True).astype(f32)
    compressed_grad, kv_gain_grad = norm_back(latent_back[:, :KV_RANK], own(compressed), own(scale_kv), gain_k)
    latent_grad = jnp.concatenate(
        [compressed_grad, unrotate(latent_back[:, KV_RANK:], own(cosine), own(sine))], axis=1
    ).astype(bf16)
    norm_grad = norm_sum + mm_nt(latent_grad, kv_down)
    input_part, attn_gain_grad = norm_back(norm_grad, own(x_float), own(scale_in), gain_a)
    input_grad = resid_grad + input_part

    q_w_grad = mm_tn(x_norm, query_grad)
    kv_up_grad = mm_tn(latent, key_grad)
    latent_grad_rows = gather(latent_grad)
    x_cols = lax.dynamic_slice_in_dim(x_norm, s * (D // S), D // S, 1)
    kv_down_grad = mm_tn(x_cols, latent_grad_rows)

    def scatter_columns(g):
        rows, cols = g.shape
        mine = lax.psum_scatter(g.astype(bf16), "expert", scatter_dimension=0, tiled=True)
        mine = lax.all_to_all(
            mine.reshape(S, rows // (E * S), cols), "shard", split_axis=0, concat_axis=0, tiled=True
        )
        return mine.transpose(1, 0, 2).reshape(rows // (E * S), S * cols).astype(f32)

    query_weight_grad = scatter_columns(q_w_grad)
    kv_up_weight_grad = scatter_columns(kv_up_grad)
    out_weight_grad = scatter_columns(out_grad)
    rows = D // (E * S)
    mine = lax.psum_scatter(kv_down_grad.astype(bf16), "expert", scatter_dimension=0, tiled=True)
    pairs = [(ee * S + ss, E * ss + ee) for ee in range(E) for ss in range(S)]
    kv_down_weight_grad = lax.ppermute(mine, BOTH, pairs).astype(f32)

    small = jnp.concatenate([router_grad, ffn_gain_grad[:, None], attn_gain_grad[:, None]], axis=1)
    small = lax.psum_scatter(small, BOTH, scatter_dimension=0, tiled=True)
    kv_gain_grad = lax.psum_scatter(kv_gain_grad, BOTH, scatter_dimension=0, tiled=True)
    return (
        block_out,
        input_grad,
        small[:, experts_all + 1],
        query_weight_grad,
        kv_down_weight_grad,
        kv_gain_grad,
        kv_up_weight_grad,
        out_weight_grad,
        small[:, experts_all],
        small[:, :experts_all],
        shared_in_grad,
        shared_down_grad,
        expert_in_grad,
        expert_down_grad,
    )


def solution(mesh):
    tokens = P(BOTH, None)
    shard = P("shard", None)
    in_specs = (
        tokens,
        tokens,
        P("expert", None),
        tokens,
        P("shard"),
        shard,
        shard,
        P("shard"),
        shard,
        shard,
        P("shard"),
        shard,
        shard,
        shard,
        P("expert", None, "shard"),
        P("expert", None, "shard"),
    )
    out_specs = (
        tokens,
        tokens,
        P(BOTH),
        tokens,
        tokens,
        P(BOTH),
        tokens,
        tokens,
        P(BOTH),
        tokens,
        tokens,
        tokens,
        P("expert", None, "shard"),
        P("expert", None, "shard"),
    )
    return jax.shard_map(local, mesh=mesh, in_specs=in_specs, out_specs=out_specs, check_vma=False)
```

time: 5160 us -> 1470 us (0.28)
  waiting for transfers between devices: 4330 us -> 539 us
  starting transfers between devices: 10.6 us -> 87.9 us
  matrix products: 371 us -> 309 us
    reduce_scatter x8, waiting for transfers between devices: 2860 us -> 35.7 us  [the longest x3 35.7 us: owners_sum(): lax.psum_scatter(part, 'shard', scatter_dimension=0, tiled=True).astype(f32)]
    all_gather x8 -> x5, waiting for transfers between devices: 1400 us -> 9.15 us  [the longest x4 9.15 us: gather(): return lax.all_gather(v, 'shard', axis=0, tiled=True)]
    ppermute x0 -> x49, waiting for transfers between devices: none -> 282 us  [the longest x48 282 us: swap(): return lax.ppermute(value, 'expert', [(i, i ^ bit) for i in range(count)])]
    all_gather x5 -> x6, blocking collectives: 80.7 us -> 239 us  [gather(): return lax.all_gather(v, 'shard', axis=0, tiled=True)]
    all_to_all x2 -> x0, blocking collectives: 105 us -> none  [the longest x1 52.7 us: local(): lax.all_to_all(send_rows, 'expert', split_axis=0, concat_axis=1, tiled=True)]
    all_to_all x2 -> x10, waiting for transfers between devices: 0.01 us -> 79.3 us  [the longest x4 73.3 us: columns_to_heads(): lax.all_to_all(parts, 'shard', split_axis=1, concat_axis=0, tiled=True)]
    dot_general x38 -> x33, matrix products: 370 us -> 309 us  [the longest x27 281 us: dot(): return lax.dot_general(a, b, (dims, ((), ())), preferred_element_type=f32)]
    unnamed x22 -> x17, waiting for transfers between devices: 73.9 us -> 132 us
  transfers between devices with their start and end apart: 21 -> 74, of which waited for: 17 -> 27; matrix products, arithmetic and copies ran while one was open for 8% -> 25% of each run, Pallas kernels for 0% -> 0%
where the time goes in v1:
time: 1470 us
  waiting for transfers between devices  539 us (37%)
  matrix products  309 us (21%)
  blocking collectives  279 us (19%)
  local copies, waits for them, and re-layouts  151 us (10%)
  starting transfers between devices  87.9 us (6%)
  other arithmetic  84.9 us (6%)
  between operations  15.8 us (1%)
    ppermute x48, waiting for transfers between devices, swap(): return lax.ppermute(value, 'expert', [(i, i ^ bit) for i in range(count)])  282 us
    dot_general x27, matrix products, dot(): return lax.dot_general(a, b, (dims, ((), ())), preferred_element_type=f32)  281 us
    all_gather x6, blocking collectives, gather(): return lax.all_gather(v, 'shard', axis=0, tiled=True)  239 us
    unnamed x17, waiting for transfers between devices  132 us
    all_to_all x4, waiting for transfers between devices, columns_to_heads(): lax.all_to_all(parts, 'shard', split_axis=1, concat_axis=0, tiled=True)  73.3 us
    unnamed x210, local copies, waits for them, and re-layouts  54.4 us
    unnamed x1, blocking collectives  40.5 us
    reduce_scatter x3, waiting for transfers between devices, owners_sum(): lax.psum_scatter(part, 'shard', scatter_dimension=0, tiled=True).astype(f32)  35.7 us
  transfers between devices with their start and end apart: 74, of which 27 were waited for; matrix products, arithmetic and copies ran while one was open for 25% of the time, Pallas kernels for 0%

profile of v1, /device:TPU:0, one launch (start us, length us, event | category | flops | bytes accessed | tf_op | source)
XLA Modules:
  0.0 1467.4 jit_solution(9078504933630943461)
XLA Ops:
  23.3 45.2 %all-to-all-done = bf16[128,4,1024]{0,2,1:T(8,128)(2,1)} async-done(((bf16[128,4,1024]{0,2,1:T(8,128)(2,1)}), bf16[128,4,1024]{0,2,1:T(8,128)(2,1)}, u32[]{:S(2)}, u32[]{:S(2)}) %all-to-all-start) | async-done | bytes 1048608 | tf_op jit(solution)/shard_map/all_to_all | solution.py:149
  73.0 73.1 %all-gather.1 = bf16[4,1,128]{2,1,0:T(2,128)(2,1)S(1)} all-gather(bf16[1,1,128]{2,1,0:T(2,128)(2,1)S(1)} %bitcast.333), channel_id=1, replica_groups=mesh['expert'=8,'shard'=4] {'shard'}, dimensions={0}, use_global_device_ids=true | all-gather | bytes 1280 | tf_op jit(solution)/shard_map/all_gather | solution.py:139
  146.1 49.3 %all-gather = bf16[4,1,512]{2,1,0:T(2,128)(2,1)S(1)} all-gather(bf16[1,1,512]{2,1,0:T(2,128)(2,1)S(1)} %reshape.443), channel_id=1, replica_groups=mesh['expert'=8,'shard'=4] {'shard'}, dimensions={0}, use_global_device_ids=true | all-gather | bytes 5120 | tf_op jit(solution)/shard_map/all_gather | solution.py:139
  262.7 18.9 %all-to-all-done.3 = bf16[512,4,88]{0,2,1:T(8,128)(2,1)S(1)} async-done(((bf16[512,4,88]{0,2,1:T(8,128)(2,1)}), bf16[512,4,88]{0,2,1:T(8,128)(2,1)S(1)}, u32[]{:S(2)}, u32[]{:S(2)}) %all-to-all-start.3) | async-done | bytes 360480 | tf_op jit(solution)/shard_map/all_to_all | solution.py:149
  286.6 36.6 %all-gather.2 = bf16[4,1,512]{2,1,0:T(2,128)(2,1)S(1)} all-gather(bf16[1,1,512]{2,1,0:T(2,128)(2,1)S(1)} %reshape.447), channel_id=1, replica_groups=mesh['expert'=8,'shard'=4] {'shard'}, dimensions={0}, use_global_device_ids=true | all-gather | bytes 5120 | tf_op jit(solution)/shard_map/all_gather | solution.py:139
  324.0 14.4 all_gather.41
  339.9 19.5 %all_gather.39 = s32[512,6]{0,1:T(8,128)S(1)} all-gather(s32[128,6]{0,1:T(8,128)S(1)} %copy-done.70), channel_id=1, replica_groups=mesh['expert'=8,'shard'=4] {'shard'}, dimensions={0}, use_global_device_ids=true | all-gather | bytes 15360 | tf_op jit(solution)/shard_map/all_gather | solution.py:139
  371.8 10.9 collective-permute-done.25
  388.3 23.8 %collective-permute-done.27 = bf16[512,2048]{1,0:T(8,128)(2,1)} collective-permute-done((bf16[512,2048]{1,0:T(8,128)(2,1)}, bf16[512,2048]{1,0:T(8,128)(2,1)}, u32[]{:S(2)}, u32[]{:S(2)}) %collective-permute-start.27) | collective-permute-done | bytes 2097184 | tf_op jit(solution)/shard_map/ppermute | solution.py:75
  419.3 14.9 %collective-permute-done.29 = bf16[512,1024]{1,0:T(8,128)(2,1)S(1)} collective-permute-done((bf16[512,1024]{1,0:T(8,128)(2,1)S(1)}, bf16[512,1024]{1,0:T(8,128)(2,1)S(1)}, u32[]{:S(2)}, u32[]{:S(2)}) %collective-permute-start.29) | collective-permute-done | bytes 1048608 | tf_op jit(solution)/shard_map/ppermute | solution.py:75
  476.5 40.7 %collective-permute-done.1 = f32[16,512]{1,0:T(8,128)S(1)} collective-permute-done((f32[16,512]{1,0:T(8,128)S(1)}, f32[16,512]{1,0:T(8,128)S(1)}, u32[]{:S(2)}, u32[]{:S(2)}) %collective-permute-start.1) | collective-permute-done | bytes 32800 | tf_op jit(solution)/shard_map/ppermute | solution.py:75
  520.7 43.6 %collective-permute-done.5 = f32[16,256]{1,0:T(8,128)S(1)} collective-permute-done((f32[16,256]{1,0:T(8,128)S(1)}, f32[16,256]{1,0:T(8,128)S(1)}, u32[]{:S(2)}, u32[]{:S(2)}) %collective-permute-start.5) | collective-permute-done | bytes 16416 | tf_op jit(solution)/shard_map/ppermute | solution.py:75
  570.6 22.0 %collective-permute-done.13 = bf16[512,1024]{1,0:T(8,128)(2,1)S(1)} collective-permute-done((bf16[512,1024]{1,0:T(8,128)(2,1)S(1)}, bf16[512,1024]{1,0:T(8,128)(2,1)S(1)}, u32[]{:S(2)}, u32[]{:S(2)}) %collective-permute-start.13) | collective-permute-done | bytes 1048608 | tf_op jit(solution)/shard_map/ppermute | solution.py:75
  598.4 46.8 %fusion.106 = f32[4096,1792]{0,1:T(8,128)} fusion(bf16[4096,2048]{1,0:T(8,128)(2,1)S(1)} %bitcast.268, bf16[2048,1792]{0,1:T(8,128)(2,1)} %broadcast_dynamic-update-slice_fusion.1), kind=kOutput, calls=%fused_computation.277 | convolution fusion | flops 30064771072 | bytes 53477376 | tf_op jit(solution)/shard_map/dot_general | solution.py:25
  651.7 37.3 %multiply_convert_fusion.1 = (bf16[4096,896]{0,1:T(8,128)(2,1)}, bf16[4096,896]{0,1:T(8,128)(2,1)}, f32[4096,896]{0,1:T(8,128)}, bf16[4096,896]{0,1:T(8,128)(2,1)}) fusion(f32[4096,1792]{0,1:T(8,128)} %fusion.106, f32[4096,352]{0,1:T(8,128)} %broadcast_in_dim.41, f32[4096,352]{0,1:T(8,128)} %broadcast_in_dim.39, f32[896]{0:T(1024)S(1)} %copy-done.71, ...), kind=kOutput, calls=%fused_computation.11 | convolution fusion | flops 15120465920 | bytes 98045440 | tf_op jit(solution)/shard_map/dot_general | solution.py:25
  689.0 37.9 %convolution_convert_fusion = bf16[4096,2048]{1,0:T(8,128)(2,1)} fusion(bf16[2048,1792]{0,1:T(8,128)(2,1)} %broadcast_dynamic-update-slice_fusion.1, bf16[4096,896]{0,1:T(8,128)(2,1)} %get-tuple-element.35, bf16[4096,896]{0,1:T(8,128)(2,1)} %get-tuple-element.34), kind=kOutput, calls=%fused_computation.1 | convolution fusion | flops 30102519808 | bytes 38797312 | tf_op jit(solution)/shard_map/dot_general | solution.py:25
  733.6 24.2 %convolution_convert_fusion.1 = bf16[4096,2048]{1,0:T(8,128)(2,1)} fusion(bf16[4096,896]{0,1:T(8,128)(2,1)} %get-tuple-element.37, bf16[2048,104]{0,1:T(8,128)(2,1)} %copy-done.42, bf16[2048,88]{0,1:T(8,128)(2,1)} %dynamic-slice_bitcast_fusion, bf16[2048,352]{0,1:T(8,128)(2,1)} %get-tuple-element.56, bf16[2048,352]{0,1:T(8,128)(2,1)S(1)} %copy-done.26), kind=kOutput, calls=%fused_computation.2 | convolution fusion | flops 15055454208 | bytes 27787264 | tf_op jit(solution)/shard_map/dot_general | solution.py:25
  778.9 17.7 %collective-permute-done.38 = bf16[512,1024]{1,0:T(8,128)(2,1)S(1)} collective-permute-done((bf16[512,1024]{1,0:T(8,128)(2,1)S(1)}, bf16[512,1024]{1,0:T(8,128)(2,1)S(1)}, u32[]{:S(2)}, u32[]{:S(2)}) %collective-permute-start.38) | collective-permute-done | bytes 1048608 | tf_op jit(solution)/shard_map/ppermute | solution.py:75
  818.8 35.8 %collective-permute-done.47 = f32[16,512]{1,0:T(8,128)S(1)} collective-permute-done((f32[16,512]{1,0:T(8,128)S(1)}, f32[16,512]{1,0:T(8,128)S(1)}, u32[]{:S(2)}, u32[]{:S(2)}) %collective-permute-start.47) | collective-permute-done | bytes 32800 | tf_op jit(solution)/shard_map/ppermute | solution.py:75
  867.6 10.8 collective-permute-done.22
  885.5 41.6 %collective-permute-done.23 = bf16[512,2048]{1,0:T(8,128)(2,1)S(1)} collective-permute-done((bf16[512,2048]{1,0:T(8,128)(2,1)S(1)}, bf16[512,2048]{1,0:T(8,128)(2,1)S(1)}, u32[]{:S(2)}, u32[]{:S(2)}) %collective-permute-start.23) | collective-permute-done | bytes 2097184 | tf_op jit(solution)/shard_map/ppermute | solution.py:75
  940.1 35.6 %reduce-scatter.15.cloned.1.call-done = bf16[128,2048]{1,0:T(8,128)(2,1)} async-done(((bf16[512,2048]{1,0:T(8,128)(2,1)}), bf16[128,2048]{1,0:T(8,128)(2,1)}) %reduce-scatter.15.cloned.1.call-update) | async-done | bytes 524304 | tf_op jit(solution)/shard_map/reduce_scatter | solution.py:303
  1001.9 20.8 %copy.172 = bf16[2048,4096]{1,0:T(8,128)(2,1)} copy(bf16[2048,4096]{0,1:T(8,128)(2,1)} %bitcast.269) | data formatting | bytes 33554432 | tf_op jit(solution)/shard_map/dot_general | solution.py:25
  1044.8 11.7 fusion.19
  1058.7 12.0 fusion.21
  1089.3 12.0 fusion.15
  1104.8 45.9 %all_gather.43 = bf16[512,576]{0,1:T(8,128)(2,1)S(1)} all-gather(bf16[128,576]{0,1:T(8,128)(2,1)S(1)} %pad_maximum_fusion.19), channel_id=1, replica_groups=mesh['expert'=8,'shard'=4] {'shard'}, dimensions={0}, use_global_device_ids=true | all-gather | bytes 737280 | tf_op jit(solution)/shard_map/all_gather | solution.py:139
  1170.5 10.7 fusion.17
  1186.2 10.8 convolution_bitcast_fusion
  1220.6 12.0 convolution_bitcast_fusion.1
  1264.1 40.5 %all-reduce = f32[512]{0:T(512)S(1)} all-reduce(f32[512]{0:T(512)S(1)} %copy-done.65), channel_id=10, replica_groups=mesh['expert'=8,'shard'=4] {'expert','shard'}, use_global_device_ids=true, to_apply=%region_29.30.clone | all-reduce | flops 512 | bytes 4096
  1326.6 129.5 %reduce-scatter.33.cloned.1.call-done = f32[64,18]{1,0:T(8,128)} async-done(((f32[2048,18]{1,0:T(8,128)}), f32[64,18]{1,0:T(8,128)}) %reduce-scatter.33.cloned.1.call-update) | async-done | bytes 4624
  (517 shorter events, 445.1 us)
Async XLA Ops:
  7.2 191.0 %all-gather.9.cloned.1.call-start = ((), (), s32[]{:S(2)}) async-start(), calls=%async_computation.20 | async-start | bytes 2621440 | tf_op jit(solution)/shard_map/all_gather | solution.py:139
  7.9 196.5 %all-gather.11.cloned.1.call-start = ((), (), s32[]{:S(2)}) async-start(), calls=%async_computation.21 | async-start | bytes 2949120 | tf_op jit(solution)/shard_map/all_gather | solution.py:139
  10.9 57.6 %all-to-all-start = ((bf16[128,4,1024]{0,2,1:T(8,128)(2,1)}), bf16[128,4,1024]{0,2,1:T(8,128)(2,1)}, u32[]{:S(2)}, u32[]{:S(2)}) async-start(bf16[128,4,1024]{0,2,1:T(8,128)(2,1)} %bitcast.3), calls=%async_computation | async-start | bytes 2097152 | tf_op jit(solution)/shard_map/all_to_all | solution.py:149
  68.5 149.6 %all-to-all-start.1 = ((bf16[512,4,768]{2,0,1:T(8,128)(2,1)}), bf16[512,4,768]{2,0,1:T(8,128)(2,1)S(1)}, u32[]{:S(2)}, u32[]{:S(2)}) async-start(bf16[512,4,768]{2,0,1:T(8,128)(2,1)} %copy.151), calls=%async_computation.1 | async-start | bytes 6291456 | tf_op jit(solution)/shard_map/all_to_all | solution.py:149
  72.2 266.2 %all-gather.17.cloned.1.call-start = ((), (), s32[]{:S(2)}) async-start(), calls=%async_computation.25 | async-start | bytes 2621440 | tf_op jit(solution)/shard_map/all_gather | solution.py:139
  72.9 377.1 %all-gather.13.cloned.1.call-start = ((), (), s32[]{:S(2)}) async-start(), calls=%async_computation.22 | async-start | bytes 2621440 | tf_op jit(solution)/shard_map/all_gather | solution.py:215
  231.4 227.8 %all-gather.15.cloned.1.call-start = ((), (), s32[]{:S(2)}) async-start(), calls=%async_computation.23 | async-start | bytes 10485760 | tf_op jit(solution)/shard_map/all_gather | solution.py:139
  282.4 100.3 %all-to-all-start.4 = ((bf16[4,88,2048]{2,1,0:T(8,128)(2,1)}), bf16[4,88,2048]{2,1,0:T(8,128)(2,1)S(1)}, u32[]{:S(2)}, u32[]{:S(2)}) async-start(bf16[4,88,2048]{2,1,0:T(8,128)(2,1)} %pad_maximum_fusion.7), calls=%async_computation.4 | async-start | bytes 2883584 | tf_op jit(solution)/shard_map/all_to_all | solution.py:169
  285.9 650.1 %reduce-scatter.19.cloned.1.call-start = ((), (), s32[]{:S(2)}) async-start(), calls=%async_computation.27 | async-start | bytes 40960 | tf_op jit(solution)/shard_map/reduce_scatter | solution.py:303
  363.4 51.2 %collective-permute-start.24 = (bf16[512,2048]{1,0:T(8,128)(2,1)}, bf16[512,2048]{1,0:T(8,128)(2,1)}, u32[]{:S(2)}, u32[]{:S(2)}) collective-permute-start(bf16[512,2048]{1,0:T(8,128)(2,1)} %all-gather.17.cloned.1.call-done), channel_id=1, source_target_pairs={{0,4},{4,0},{8,12},{12,8},{16,20},{20,16},{24,28},{28,24},{1,5},{5... | collective-permute-start | bytes 6291464 | tf_op jit(solution)/shard_map/ppermute | solution.py:75
  363.4 48.7 %collective-permute-start.27 = (bf16[512,2048]{1,0:T(8,128)(2,1)}, bf16[512,2048]{1,0:T(8,128)(2,1)}, u32[]{:S(2)}, u32[]{:S(2)}) collective-permute-start(bf16[512,2048]{1,0:T(8,128)(2,1)} %all-gather.17.cloned.1.call-done), channel_id=1, source_target_pairs={{0,16},{4,20},{8,24},{12,28},{16,0},{20,4},{24,8},{28,12},{1,17},{... | collective-permute-start | bytes 6291464 | tf_op jit(solution)/shard_map/ppermute | solution.py:75
  382.6 56.3 %collective-permute-start.26 = (bf16[512,2048]{1,0:T(8,128)(2,1)S(1)}, bf16[512,2048]{1,0:T(8,128)(2,1)}, u32[]{:S(2)}, u32[]{:S(2)}) collective-permute-start(bf16[512,2048]{1,0:T(8,128)(2,1)S(1)} %collective-permute-done.25), channel_id=1, source_target_pairs={{0,4},{4,0},{8,12},{12,8},{16,20},{20,16},{24,28},{28,24},{1,5},{5... | collective-permute-start | bytes 6291464 | tf_op jit(solution)/shard_map/ppermute | solution.py:75
  386.6 47.5 %collective-permute-start.29 = (bf16[512,1024]{1,0:T(8,128)(2,1)S(1)}, bf16[512,1024]{1,0:T(8,128)(2,1)S(1)}, u32[]{:S(2)}, u32[]{:S(2)}) collective-permute-start(bf16[512,1024]{1,0:T(8,128)(2,1)S(1)} %slice.423), channel_id=1, source_target_pairs={{0,16},{4,20},{8,24},{12,28},{16,0},{20,4},{24,8},{28,12},{1,17},{... | collective-permute-start | bytes 3145736 | tf_op jit(solution)/shard_map/ppermute | solution.py:75
  468.9 97.8 %collective-permute-start.9 = (bf16[512,2048]{1,0:T(8,128)(2,1)S(1)}, bf16[512,2048]{1,0:T(8,128)(2,1)S(1)}, u32[]{:S(2)}, u32[]{:S(2)}) collective-permute-start(bf16[512,2048]{1,0:T(8,128)(2,1)S(1)} %get-tuple-element.31), channel_id=1, source_target_pairs={{0,8},{4,12},{8,0},{12,4},{16,24},{20,28},{24,16},{28,20},{1,9},{5... | collective-permute-start | bytes 6291464 | tf_op jit(solution)/shard_map/ppermute | solution.py:75
  471.1 48.1 %collective-permute-start = (f32[16,512]{1,0:T(8,128)S(1)}, f32[16,512]{1,0:T(8,128)S(1)}, u32[]{:S(2)}, u32[]{:S(2)}) collective-permute-start(f32[16,512]{1,0:T(8,128)S(1)} %bitcast.316), channel_id=1, source_target_pairs={{0,4},{4,0},{8,12},{12,8},{16,20},{20,16},{24,28},{28,24},{1,5},{5... | collective-permute-start | bytes 98312 | tf_op jit(solution)/shard_map/ppermute | solution.py:75
  476.5 93.8 %collective-permute-start.8 = (bf16[512,2048]{1,0:T(8,128)(2,1)S(1)}, bf16[512,2048]{1,0:T(8,128)(2,1)S(1)}, u32[]{:S(2)}, u32[]{:S(2)}) collective-permute-start(bf16[512,2048]{1,0:T(8,128)(2,1)S(1)} %get-tuple-element.31), channel_id=1, source_target_pairs={{0,4},{4,0},{8,12},{12,8},{16,20},{20,16},{24,28},{28,24},{1,5},{5... | collective-permute-start | bytes 6291464 | tf_op jit(solution)/shard_map/ppermute | solution.py:75
  517.2 51.5 %collective-permute-start.11 = (bf16[512,2048]{1,0:T(8,128)(2,1)S(1)}, bf16[512,2048]{1,0:T(8,128)(2,1)S(1)}, u32[]{:S(2)}, u32[]{:S(2)}) collective-permute-start(bf16[512,2048]{1,0:T(8,128)(2,1)S(1)} %get-tuple-element.31), channel_id=1, source_target_pairs={{0,16},{4,20},{8,24},{12,28},{16,0},{20,4},{24,8},{28,12},{1,17},{... | collective-permute-start | bytes 6291464 | tf_op jit(solution)/shard_map/ppermute | solution.py:75
  805.6 52.0 %collective-permute-start.32 = (bf16[512,2048]{1,0:T(8,128)(2,1)}, bf16[512,2048]{1,0:T(8,128)(2,1)S(1)}, u32[]{:S(2)}, u32[]{:S(2)}) collective-permute-start(bf16[512,2048]{1,0:T(8,128)(2,1)} %get-tuple-element.38), channel_id=1, source_target_pairs={{0,4},{4,0},{8,12},{12,8},{16,20},{20,16},{24,28},{28,24},{1,5},{5... | collective-permute-start | bytes 6291464 | tf_op jit(solution)/shard_map/ppermute | solution.py:75
  806.9 50.7 %collective-permute-start.39 = (bf16[512,2048]{1,0:T(8,128)(2,1)}, bf16[512,2048]{1,0:T(8,128)(2,1)}, u32[]{:S(2)}, u32[]{:S(2)}) collective-permute-start(bf16[512,2048]{1,0:T(8,128)(2,1)} %pad_maximum_fusion.6), channel_id=1, source_target_pairs={{0,16},{4,20},{8,24},{12,28},{16,0},{20,4},{24,8},{28,12},{1,17},{... | collective-permute-start | bytes 6291464 | tf_op jit(solution)/shard_map/ppermute | solution.py:75
  807.5 50.1 %collective-permute-start.36 = (bf16[512,2048]{1,0:T(8,128)(2,1)}, bf16[512,2048]{1,0:T(8,128)(2,1)}, u32[]{:S(2)}, u32[]{:S(2)}) collective-permute-start(bf16[512,2048]{1,0:T(8,128)(2,1)} %pad_maximum_fusion.5), channel_id=1, source_target_pairs={{0,8},{4,12},{8,0},{12,4},{16,24},{20,28},{24,16},{28,20},{1,9},{5... | collective-permute-start | bytes 6291464 | tf_op jit(solution)/shard_map/ppermute | solution.py:75
  856.5 81.0 %reduce-scatter.17.cloned.1.call-start = ((), (), s32[]{:S(2)}) async-start(), calls=%async_computation.26 | async-start | bytes 2621440 | tf_op jit(solution)/shard_map/reduce_scatter | solution.py:303
  863.6 112.1 %reduce-scatter.15.cloned.1.call-start = ((), (), s32[]{:S(2)}) async-start(), calls=%async_computation.24 | async-start | bytes 2621440 | tf_op jit(solution)/shard_map/reduce_scatter | solution.py:303
  993.2 108.0 %reduce-scatter.31.cloned.1.call-start = ((), (), s32[]{:S(2)}) async-start(), calls=%async_computation.33 | async-start | bytes 819200
  1044.8 187.8 %reduce-scatter.27.cloned.1.call-start = ((), (), s32[]{:S(2)}) async-start(), calls=%async_computation.31 | async-start | bytes 1179648 | tf_op jit(solution)/shard_map/reduce_scatter | solution.py:364
  1058.3 192.0 %reduce-scatter.29.cloned.1.call-start = ((), (), s32[]{:S(2)}) async-start(), calls=%async_computation.32 | async-start | bytes 2359296 | tf_op jit(solution)/shard_map/reduce_scatter | solution.py:364
  1083.1 149.5 %all-to-all-start.9 = ((f32[32,64,176]{2,1,0:T(8,128)}), f32[32,64,176]{2,1,0:T(8,128)}, u32[]{:S(2)}, u32[]{:S(2)}) async-start(f32[32,64,176]{2,1,0:T(8,128)} %fusion.43), calls=%async_computation.17 | async-start | bytes 4194304 | tf_op jit(solution)/shard_map/all_to_all | solution.py:294
  1089.2 216.0 %reduce-scatter.25.cloned.1.call-start = ((), (), s32[]{:S(2)}) async-start(), calls=%async_computation.30 | async-start | bytes 737280 | tf_op jit(solution)/shard_map/reduce_scatter | solution.py:374
  1153.2 155.8 %reduce-scatter.21.cloned.1.call-start = ((), (), s32[]{:S(2)}) async-start(), calls=%async_computation.28 | async-start | bytes 2621440 | tf_op jit(solution)/shard_map/reduce_scatter | solution.py:347
  1170.2 143.3 %reduce-scatter.23.cloned.1.call-start = ((), (), s32[]{:S(2)}) async-start(), calls=%async_computation.29 | async-start | bytes 3538944 | tf_op jit(solution)/shard_map/reduce_scatter | solution.py:364
  1250.3 57.9 %all-to-all-start.8 = ((bf16[4,64,512]{2,1,0:T(8,128)(2,1)}), bf16[4,64,512]{2,1,0:T(8,128)(2,1)S(1)}, u32[]{:S(2)}, u32[]{:S(2)}) async-start(bf16[4,64,512]{2,1,0:T(8,128)(2,1)} %bitcast.306), calls=%async_computation.16 | async-start | bytes 524288 | tf_op jit(solution)/shard_map/all_to_all | solution.py:365
  1253.7 202.4 %reduce-scatter.33.cloned.1.call-start = ((), (), s32[]{:S(2)}) async-start(), calls=%async_computation.34 | async-start | bytes 1081344
  1313.6 146.1 %all-to-all-start.6 = ((bf16[4,64,768]{2,1,0:T(8,128)(2,1)}), bf16[4,64,768]{2,1,0:T(8,128)(2,1)S(1)}, u32[]{:S(2)}, u32[]{:S(2)}) async-start(bf16[4,64,768]{2,1,0:T(8,128)(2,1)} %bitcast.304), calls=%async_computation.11 | async-start | bytes 786432 | tf_op jit(solution)/shard_map/all_to_all | solution.py:365
  (125 other events, 2952.3 us)
Sparse Core Ops, SparseCore 0:
  9.6 87.6 all-gather.8
  98.8 83.0 all-gather.10
  183.6 44.1 all-gather.16
  231.5 72.7 all-gather.12
  305.7 153.4 all-gather.14
  856.6 16.4 reduce-scatter.18
  875.5 42.0 reduce-scatter.16
  935.3 40.3 reduce-scatter.14
  1044.9 23.4 reduce-scatter.30
  1072.3 46.7 reduce-scatter.26
  1122.7 42.5 reduce-scatter.28
  1168.3 34.5 reduce-scatter.24
  1205.2 45.9 reduce-scatter.20
  1254.8 45.7 reduce-scatter.22
  1313.7 142.4 reduce-scatter.32

commit v2 on v1

v2 whole, which is shorter than its diff:
```python
import functools

import jax
import jax.numpy as jnp
from jax import lax
from jax.experimental import pallas as pl
from jax.experimental.pallas import tpu as pltpu
from jax.sharding import PartitionSpec as P

D = 2048
HEADS = 16
NOPE = 128
ROPE = 64
VDIM = 128
QK = NOPE + ROPE
KV_RANK = 512
SH_FF = 2816
EXP_DEV = 2
FF_PAD = 896

EPS = 1e-06
ROPE_BASE = 10000.0
BOTH = ("expert", "shard")
bf16 = jnp.bfloat16
f32 = jnp.float32


def dot(a, b, dims):
    return lax.dot_general(a, b, (dims, ((), ())), preferred_element_type=f32)


def mm(a, b):
    return dot(a, b, ((1,), (0,)))


def mm_tn(a, b):
    return dot(a, b, ((0,), (0,)))


def mm_nt(a, b):
    return dot(a, b, ((1,), (1,)))


def inv_rms(values):
    return lax.rsqrt(jnp.mean(values * values, axis=-1, keepdims=True) + EPS)


def norm_back(grad_out, values, inv_scale, gain_row):
    scaled = grad_out * gain_row
    grad_in = inv_scale * scaled - values * inv_scale**3 * jnp.mean(
        scaled * values, axis=-1, keepdims=True
    )
    grad_gain = jnp.sum(grad_out * values * inv_scale, axis=0)
    return (grad_in, grad_gain)


def rope_tables(doc_row):
    count = doc_row.shape[0]
    index = jnp.arange(count, dtype=jnp.int32)
    before = (doc_row[:, None] == doc_row[None, :]) & (index[None, :] < index[:, None])
    positions = jnp.sum(before.astype(f32), axis=1)
    half = ROPE // 2
    frequency = ROPE_BASE ** (-jnp.arange(half, dtype=f32) / half)
    angles = positions[:, None] * frequency[None, :]
    return (jnp.cos(angles), jnp.sin(angles))


def rotate(values, cosine, sine):
    half = cosine.shape[-1]
    a, b = values[..., :half], values[..., half:]
    return jnp.concatenate([a * cosine - b * sine, b * cosine + a * sine], axis=-1)


def unrotate(values, cosine, sine):
    return rotate(values, cosine, -sine)


def flip(index, bit):
    return index + bit - 2 * bit * ((index // bit) % 2)


ANY = pl.BlockSpec(memory_space=pl.ANY)
MESH = pl.DeviceIdType.MESH


def remote(src, dst, send, recv, **where):
    return pltpu.make_async_remote_copy(
        src_ref=src, dst_ref=dst, send_sem=send, recv_sem=recv, device_id=where, device_id_type=MESH
    )


def greet(peers):
    barrier = pltpu.get_barrier_semaphore()
    for where in peers:
        pl.semaphore_signal(barrier, inc=1, device_id=where, device_id_type=MESH)
    pl.semaphore_wait(barrier, len(peers))


def exchange_views(kind, src, dst, S):
    if kind == "rows":
        r = src.shape[0]
        return (lambda t: src), (lambda q: dst.at[pl.ds(q * r, r)])
    if kind == "cols":
        c = src.shape[1]
        return (lambda t: src), (lambda q: dst.at[:, pl.ds(q * c, c)])
    if kind == "cols_to_rows":
        r, c = src.shape[0], src.shape[1] // S
        return (lambda t: src.at[:, pl.ds(t * c, c)]), (lambda q: dst.at[pl.ds(q * r, r)])
    if kind == "rows_to_cols":
        r, c = src.shape[0] // S, src.shape[1]
        return (lambda t: src.at[pl.ds(t * r, r)]), (lambda q: dst.at[:, pl.ds(q * c, c)])
    r = src.shape[0] // S
    return (lambda t: src.at[pl.ds(t * r, r)]), (lambda q: dst.at[pl.ds(q * r, r)])


def exchange_shape(kind, a, S):
    r, c = a.shape
    return {
        "rows": (S * r, c),
        "cols": (r, S * c),
        "cols_to_rows": (S * r, c // S),
        "rows_to_cols": (r // S, S * c),
        "blocks": (r, c),
    }[kind]


def shard_exchange(ident, S, *items):
    count = len(items)

    def kernel(*refs):
        ins, outs = refs[:count], refs[count : 2 * count]
        send, recv, here = refs[2 * count :]
        me = lax.axis_index("shard")
        greet([{"shard": lax.rem(me + k, S)} for k in range(1, S)])
        waits = []
        for i, (kind, _) in enumerate(items):
            out_of, into = exchange_views(kind, ins[i], outs[i], S)
            for k in range(1, S):
                to = lax.rem(me + k, S)
                waits.append(remote(out_of(to), into(me), send.at[i, k], recv.at[i, k], shard=to))
                waits[-1].start()
            waits.append(pltpu.make_async_copy(out_of(me), into(me), here.at[i]))
            waits[-1].start()
        for copy in waits:
            copy.wait()

    return pl.pallas_call(
        kernel,
        out_shape=[jax.ShapeDtypeStruct(exchange_shape(kind, a, S), a.dtype) for kind, a in items],
        in_specs=[ANY] * count,
        out_specs=[ANY] * count,
        scratch_shapes=[
            pltpu.SemaphoreType.DMA((count, S)),
            pltpu.SemaphoreType.DMA((count, S)),
            pltpu.SemaphoreType.DMA((count,)),
        ],
        compiler_params=pltpu.CompilerParams(collective_id=ident, has_side_effects=True),
    )(*[a for _, a in items])


def fetch_weights(ident, E, S, x, small, weights):
    chips = E // 2
    shaped = []
    for w, split in weights:
        r, c = w.shape
        shaped.append((w.reshape(chips, 2, r // E, c), c // S if split else c))
    count = len(weights)

    def kernel(*refs):
        x_ref, s_ref = refs[:2]
        w_refs = refs[2 : 2 + count]
        xo_ref, so_ref = refs[2 + count : 4 + count]
        o_refs = refs[4 + count : 4 + 2 * count]
        zs, zr, ps, pr, cs, cr, here = refs[4 + 2 * count :]
        me, e = lax.axis_index("shard"), lax.axis_index("expert")
        chip, core = e // 2, lax.rem(e, 2)
        greet(
            [{"shard": lax.rem(me + k, S)} for k in range(1, S)]
            + [{"expert": lax.rem(e + 2 * m, E)} for m in range(1, chips)]
            + [{"expert": flip(e, 1)}]
        )
        sent, got = [], []
        locals_ = []

        def z_copy(i, k, src, dst):
            copy = remote(src, dst, zs.at[i, k], zr.at[i, k], shard=lax.rem(me - k + S, S))
            copy.start()
            return copy

        def columns(i, t):
            c = shaped[i][1]
            if weights[i][1]:
                return w_refs[i].at[:, :, :, pl.ds(t * c, c)]
            return w_refs[i]

        def piece(i, t):
            c = shaped[i][1]
            if weights[i][1]:
                return w_refs[i].at[chip, core, :, pl.ds(t * c, c)]
            return w_refs[i].at[chip, core]

        z_waits = {}
        rows_x, rows_s = x_ref.shape[0], s_ref.shape[0]
        for k in range(1, S):
            to = lax.rem(me - k + S, S)
            for i in range(count):
                z_waits[i, k] = z_copy(i, k, piece(i, to), o_refs[i].at[me, chip, core])
        for k in range(1, S):
            z_waits["x", k] = z_copy(count, k, x_ref, xo_ref.at[pl.ds(me * rows_x, rows_x)])
            z_waits["s", k] = z_copy(count + 1, k, s_ref, so_ref.at[pl.ds(me * rows_s, rows_s)])
        for i in range(count):
            locals_.append(pltpu.make_async_copy(columns(i, me), o_refs[i].at[me], here.at[i]))
        locals_.append(pltpu.make_async_copy(x_ref, xo_ref.at[pl.ds(me * rows_x, rows_x)], here.at[count]))
        locals_.append(pltpu.make_async_copy(s_ref, so_ref.at[pl.ds(me * rows_s, rows_s)], here.at[count + 1]))
        for copy in locals_:
            copy.start()
        plane = []
        for k in range(1, S):
            q = lax.rem(me + k, S)
            for i in range(count):
                z_waits[i, k].wait_recv()
                at = o_refs[i].at[q, chip, core]
                for m in range(1, chips):
                    copy = remote(at, at, ps.at[i, k, m], pr.at[i, k, m], expert=lax.rem(e + 2 * m, E))
                    copy.start()
                    plane.append((i, k, m, copy))
        last = []
        for k in range(1, S):
            q = lax.rem(me + k, S)
            for i in range(count):
                for i2, k2, m, copy in plane:
                    if (i2, k2) == (i, k):
                        copy.wait_recv()
                at = o_refs[i].at[q, :, core]
                copy = remote(at, at, cs.at[i, k], cr.at[i, k], expert=flip(e, 1))
                copy.start()
                last.append(copy)
        for k in range(1, S):
            z_waits["x", k].wait_recv()
            z_waits["s", k].wait_recv()
        for copy in last:
            copy.wait()
        for copy in z_waits.values():
            copy.wait_send()
        for entry in plane:
            entry[3].wait_send()
        for copy in locals_:
            copy.wait()

    dma = pltpu.SemaphoreType.DMA
    outs = pl.pallas_call(
        kernel,
        out_shape=[jax.ShapeDtypeStruct((S * v.shape[0], v.shape[1]), v.dtype) for v in (x, small)]
        + [jax.ShapeDtypeStruct((S,) + v.shape[:3] + (c,), v.dtype) for v, c in shaped],
        in_specs=[ANY] * (2 + count),
        out_specs=[ANY] * (2 + count),
        scratch_shapes=[
            dma((count + 2, S)),
            dma((count + 2, S)),
            dma((count, S, chips)),
            dma((count, S, chips)),
            dma((count, S)),
            dma((count, S)),
            dma((count + 2,)),
        ],
        compiler_params=pltpu.CompilerParams(collective_id=ident, has_side_effects=True),
    )(x, small, *[v for v, _ in shaped])
    return list(outs[:2]) + [o.reshape(-1, o.shape[-1]) for o in outs[2:]]


def shared_rows(v, count):
    rows, halves = v.shape[0], v.shape[1] // 2
    width = -(-(count + 127) // 128) * 128

    def kernel(v_ref, o_ref, window, sems):
        first = lax.axis_index("expert") * count
        start = jnp.minimum(first // 128, (halves - width) // 128) * 128
        loads = [
            pltpu.make_async_copy(
                v_ref.at[:, pl.ds(pl.multiple_of(j * halves + start, 128), width)], window.at[j], sems.at[j]
            )
            for j in range(2)
        ]
        for copy in loads:
            copy.start()
        for j in range(2):
            loads[j].wait()
            turned = pltpu.roll(window[j].astype(f32), lax.rem(width - (first - start), width), 1)
            o_ref[j] = turned.T[:count].astype(bf16)

    return pl.pallas_call(
        kernel,
        out_shape=jax.ShapeDtypeStruct((2, count, rows), bf16),
        in_specs=[ANY],
        out_specs=pl.BlockSpec(memory_space=pltpu.VMEM),
        scratch_shapes=[pltpu.VMEM((2, rows, width), bf16), pltpu.SemaphoreType.DMA((2,))],
        compiler_params=pltpu.CompilerParams(vmem_limit_bytes=16 * 2**20),
    )(v)


def add_into(dst, rows, *terms):
    step = 16

    @pl.loop(0, rows // step)
    def _(i):
        at = pl.ds(pl.multiple_of(i * step, step), step)
        total = terms[0][at, :].astype(f32)
        for term in terms[1:]:
            total = total + term[at, :].astype(f32)
        dst[at, :] = total.astype(dst.dtype)


class PlaneSum:
    SEMS = 4 + 4 + 4 + 2 + 2 + 2 + 2

    @staticmethod
    def scratch(rows, cols):
        return [
            pltpu.VMEM((4, rows, cols), bf16),
            pltpu.VMEM((4, rows, cols), bf16),
            pltpu.VMEM((2, rows // 2, cols), bf16),
            pltpu.VMEM((2, rows, cols), bf16),
            pltpu.SemaphoreType.DMA((PlaneSum.SEMS,)),
        ]

    def __init__(self, term, mine, core, diag, side, sems, e):
        self.term, self.mine, self.core, self.diag, self.side, self.sems = term, mine, core, diag, side, sems
        self.rows = mine.shape[1]
        self.ec, self.ex, self.ey = flip(e, 1), flip(e, 2), flip(e, 4)
        self.at = [e, self.ex, self.ey, flip(self.ex, 4)]

    def start(self):
        self.loads = [pltpu.make_async_copy(self.term(i), self.mine.at[j], self.sems.at[j]) for j, i in enumerate(self.at)]
        self.cores = [
            remote(self.term(flip(i, 1)), self.core.at[j], self.sems.at[4 + j], self.sems.at[8 + j], expert=self.ec)
            for j, i in enumerate(self.at)
        ]
        for j in (3, 1, 2, 0):
            self.cores[j].start()
            self.loads[j].start()

    def send_diagonal(self):
        half = self.rows // 2
        self.loads[3].wait()
        self.cores[3].wait_recv()
        add_into(self.mine.at[3], self.rows, self.mine.at[3], self.core.at[3])
        low, high = self.mine.at[3, pl.ds(0, half)], self.mine.at[3, pl.ds(half, half)]
        self.diags = [
            remote(low, self.diag.at[0], self.sems.at[12], self.sems.at[14], expert=self.ex),
            remote(high, self.diag.at[1], self.sems.at[13], self.sems.at[15], expert=self.ey),
        ]
        for copy in self.diags:
            copy.start()

    def send_sides(self):
        half = self.rows // 2
        for j in (1, 2):
            self.loads[j].wait()
            self.cores[j].wait_recv()
        low, high = pl.ds(0, half), pl.ds(half, half)
        mine, core, diag = self.mine, self.core, self.diag
        add_into(mine.at[1, low], half, mine.at[1, low], core.at[1, low])
        add_into(mine.at[2, high], half, mine.at[2, high], core.at[2, high])
        self.diags[1].wait_recv()
        add_into(mine.at[1, high], half, mine.at[1, high], core.at[1, high], diag.at[1])
        self.sides = [remote(mine.at[1], self.side.at[0], self.sems.at[16], self.sems.at[18], expert=self.ex)]
        self.sides[0].start()
        self.diags[0].wait_recv()
        add_into(mine.at[2, low], half, mine.at[2, low], core.at[2, low], diag.at[0])
        self.sides.append(remote(mine.at[2], self.side.at[1], self.sems.at[17], self.sems.at[19], expert=self.ey))
        self.sides[1].start()

    def finish(self):
        self.loads[0].wait()
        self.cores[0].wait_recv()
        self.sides[0].wait_recv()
        self.sides[1].wait_recv()
        mine = self.mine.at[0]
        add_into(mine, self.rows, mine, self.core.at[0], self.side.at[0], self.side.at[1])
        for copy in self.cores + self.diags + self.sides:
            copy.wait_send()
        return mine


def reduce_weights(ident, E, S, chunks, extra):
    n, m = len(chunks), len(extra)
    arrays = []
    for a, _ in chunks:
        if not any(a is v for v in arrays):
            arrays.append(a)
    index = [next(i for i, v in enumerate(arrays) if v is a) for a, _ in chunks]
    u = len(arrays)

    def out_shape(a, kind):
        r, c = a.shape[-2:]
        if kind == "keep" or isinstance(kind, int):
            return (r, c)
        return exchange_shape(kind, jax.ShapeDtypeStruct((r, c), a.dtype), S)

    by_plane = any(kind == "plane" for kind, _ in extra)

    def kernel(*refs):
        ins, more = refs[:u], refs[u : u + m]
        outs, more_outs = refs[u + m : u + m + n], refs[u + m + n : u + n + 2 * m]
        scratch = refs[u + n + 2 * m : -3]
        send, recv, here = refs[-3:]
        me, e = lax.axis_index("shard"), lax.axis_index("expert")
        greet(
            [{"shard": lax.rem(me + k, S)} for k in range(1, S)]
            + [{"expert": lax.rem(e + k, E)} for k in range(1, E) if by_plane]
            + [{"expert": flip(e, bit)} for bit in (1, 2, 4) if not by_plane]
        )

        def term_of(j):
            ref, kind = ins[index[j]], chunks[j][1]
            if isinstance(kind, int):
                return lambda i: ref.at[i, lax.rem(me + kind, S)]
            return lambda i: ref.at[i]

        sums = [PlaneSum(term_of(j), *scratch[5 * j : 5 * j + 5], e) for j in range(n)]
        waits = []

        def spread(slot, kind, src, dst):
            out_of, into = exchange_views(kind, src, dst, S)
            for k in range(1, S):
                to = lax.rem(me + k, S)
                waits.append(remote(out_of(to), into(me), send.at[slot, k], recv.at[slot, k], shard=to))
                waits[-1].start()
            waits.append(pltpu.make_async_copy(out_of(me), into(me), here.at[slot]))
            waits[-1].start()

        def deliver(j):
            total, kind = sums[j].finish(), chunks[j][1]
            if kind == "keep" or (isinstance(kind, int) and kind == 0):
                waits.append(pltpu.make_async_copy(total, outs[j], here.at[j]))
                waits[-1].start()
            elif isinstance(kind, int):
                to = lax.rem(me + kind, S)
                waits.append(remote(total, outs[j], send.at[j, kind], recv.at[j, kind], shard=to))
                waits[-1].start()
            else:
                spread(j, kind, total, outs[j])

        for i, (kind, _) in enumerate(extra):
            if kind != "plane":
                spread(n + i, kind, more[i], more_outs[i])
                continue
            for k in range(1, E):
                to = lax.rem(e + k, E)
                waits.append(remote(more[i].at[to], more_outs[i].at[e], send.at[n + i, k], recv.at[n + i, k], expert=to))
                waits[-1].start()
            waits.append(pltpu.make_async_copy(more[i].at[e], more_outs[i].at[e], here.at[n + i]))
            waits[-1].start()
        for each in sums:
            each.start()
        for each in sums:
            each.send_diagonal()
        for each in sums:
            each.send_sides()
        for j in range(n):
            deliver(j)
        for copy in waits:
            copy.wait()

    scratch = []
    for a, _ in chunks:
        scratch += PlaneSum.scratch(*a.shape[-2:])
    dma = pltpu.SemaphoreType.DMA
    return pl.pallas_call(
        kernel,
        out_shape=[jax.ShapeDtypeStruct(out_shape(a, kind), a.dtype) for a, kind in chunks]
        + [
            jax.ShapeDtypeStruct(a.shape if kind == "plane" else exchange_shape(kind, a, S), a.dtype)
            for kind, a in extra
        ],
        in_specs=[ANY] * (u + m),
        out_specs=[ANY] * (n + m),
        scratch_shapes=scratch + [dma((n + m, max(S, E))), dma((n + m, max(S, E))), dma((n + m,))],
        compiler_params=pltpu.CompilerParams(
            collective_id=ident, has_side_effects=True, vmem_limit_bytes=48 * 2**20
        ),
    )(*arrays, *[a for _, a in extra])


def hidden_kernel(ident, S, h_side, cot_all, w_exp, w_sh, d_exp, d_sh, shared):
    rows, wide = h_side.shape
    cols = FF_PAD
    T = 2 * rows
    side = wide - D
    hot = 8 * EXP_DEV
    ff = w_exp.shape[1]
    both = EXP_DEV * ff
    rest = cols - both

    def kernel(
        h_ref, c_all, we_hbm, ws_hbm, de_hbm, ds_hbm,
        h_all, out_all, back_sum, in_grad, down_grad, sh_grad, sd_grad,
        wi, wd, acc_in, acc_down, hv, cv, pre, mg, mid, pg, ov, aside,
        mine, stage, core_in, diag_in, side_in, cut,
        send, recv, load, store, fixed, sum_send, sum_recv,
    ):
        me, e = lax.axis_index("shard"), lax.axis_index("expert")
        ec, ex, ey = flip(e, 1), flip(e, 2), flip(e, 4)
        exy = flip(ex, 4)
        greet(
            [{"shard": lax.rem(me + k, S)} for k in range(1, S)]
            + [{"expert": ec}, {"expert": ex}, {"expert": ey}]
        )

        def pull(kind, k, src, at, **where):
            return remote(src, at, send.at[kind, k], recv.at[kind, k], **where)

        def z_copy(k):
            return pull(0, k, h_ref, h_all.at[e, me], shard=lax.rem(me - k + S, S))

        def block(at, k):
            return h_all.at[at, lax.rem(me + k, S)]

        def hop(kind, k):
            if kind in (1, 2, 3):
                at = block(e, k)
                return pull(kind, k, at, at, expert={1: ec, 2: ex, 3: ey}[kind])
            at = block({4: ex, 5: ey, 7: exy}[kind], k)
            return pull(kind, k, at, at, expert=ec)

        def diag(k, by_x):
            at = block(ex if by_x else ey, k)
            return pull(6, k, at, at, expert=ey if by_x else ex)

        own = pltpu.make_async_copy(h_ref, h_all.at[e, me], fixed.at[0])
        def expert_rows(hbm, hbm_down, rows_in, rows_down):
            made = []
            for x in range(EXP_DEV):
                made.append((hbm.at[x, :, pl.ds(0, D)], rows_in.at[pl.ds(x * ff, ff)]))
                made.append((hbm.at[x, :, pl.ds(D, D)], rows_in.at[pl.ds(cols + x * ff, ff)]))
                made.append((hbm_down.at[x], rows_down.at[pl.ds(x * ff, ff)]))
            return made

        loads = expert_rows(we_hbm, de_hbm, wi, wd) + [
            (ws_hbm.at[0], wi.at[pl.ds(both, rest)]),
            (ws_hbm.at[1], wi.at[pl.ds(cols + both, rest)]),
            (ds_hbm, wd.at[pl.ds(both, rest)]),
        ]
        weights = [pltpu.make_async_copy(src, dst, fixed.at[1 + i]) for i, (src, dst) in enumerate(loads)]
        own.start()
        z_copy(1).start()
        for copy in weights:
            copy.start()

        @pl.loop(0, cols // 32)
        def _(i):
            acc_in[pl.ds(pl.multiple_of(i * 64, 64), 64), :] = jnp.zeros((64, D), f32)
            acc_down[pl.ds(pl.multiple_of(i * 32, 32), 32), :] = jnp.zeros((32, D), f32)

        own.wait()

        def out_copies(at, to, k):
            q = lax.rem(me + k, S)
            return [
                pltpu.make_async_copy(ov.at[pl.ds(j * rows, rows)], out_all.at[index, q], store.at[j])
                for j, index in enumerate((at, to))
            ]

        def weight_grads(slot):
            for m in range(2):
                part = pl.ds(m * cols, cols)
                acc_in[part, :] += mm_tn(pg[:, part], hv[slot, :, :D])
            acc_down[...] += mm_tn(mid[...], cv[slot])

        def plane(at, src, dst, **where):
            return remote(src, dst, sum_send.at[at], sum_recv.at[at], **where)

        def to_core(u):
            return plane(u % 2, stage.at[u % 2], core_in.at[u % 2], expert=ec)

        half = rows // 2
        first_half, last_half = pl.ds(0, half), pl.ds(half, half)

        def diagonals(j):
            term = mine.at[j % 2, 3]
            return [
                plane(2, term.at[first_half], diag_in.at[0], expert=ex),
                plane(3, term.at[last_half], diag_in.at[1], expert=ey),
            ]

        def sides(j):
            return [
                plane(4, mine.at[j % 2, 1], side_in.at[0], expert=ex),
                plane(5, mine.at[j % 2, 2], side_in.at[1], expert=ey),
            ]

        def to_owner(j):
            k = chunk(j)
            return plane(6 + k, mine.at[j % 2, 0], back_sum.at[k], shard=lax.rem(me + k, S))

        def add_core(w):
            to_core(w).wait_recv()
            term = mine.at[(w // 4) % 2, w % 4]
            add_into(term, rows, term, core_in.at[w % 2])

        def send_diagonals(j):
            for copy in diagonals(j):
                copy.start()

        def send_sides(j):
            for copy in diagonals(j):
                copy.wait_recv()
            by_x, by_y = mine.at[j % 2, 1, last_half], mine.at[j % 2, 2, first_half]
            add_into(by_x, half, by_x, diag_in.at[1])
            add_into(by_y, half, by_y, diag_in.at[0])
            for copy in sides(j):
                copy.start()

        def finish_sum(j):
            for copy in sides(j):
                copy.wait_recv()
            total = mine.at[j % 2, 0]
            add_into(total, rows, total, side_in.at[0], side_in.at[1])
            for copy in diagonals(j) + sides(j):
                copy.wait_send()

        def unit(at, to, k, u, began):
            q = lax.rem(me + k, S)
            slot = u % 2
            loads = [
                [
                    pltpu.make_async_copy(
                        (h_all, c_all)[a].at[index, q],
                        (hv, cv)[a].at[slot, pl.ds(j * rows, rows)],
                        load.at[a, j],
                    )
                    for j, index in enumerate((at, to))
                ]
                for a in range(2)
            ]
            for pair in loads:
                for copy in pair:
                    copy.start()

            @pl.when(began)
            def _():
                weight_grads(1 - slot)

            for pair in loads:
                for copy in pair:
                    copy.wait()
            pre[...] = mm_nt(hv[slot, :, :D], wi[...])
            mg[...] = mm_nt(cv[slot], wd[...])

            @pl.when(began)
            def _():
                for copy in out_copies(at, to, k):
                    copy.wait()

            step = 64

            @pl.loop(0, T // step)
            def _(i):
                part = pl.ds(pl.multiple_of(i * step, step), step)
                lane = lax.broadcasted_iota(jnp.int32, (step, side), 1)
                w_side = hv[slot, part, D:].astype(f32)

                def weight(x):
                    keep = (lane == EXP_DEV * e + x) | (lane == hot + EXP_DEV * e + x)
                    return jnp.sum(jnp.where(keep, w_side, 0.0), axis=1, keepdims=True)

                w = [weight(x) for x in range(EXP_DEV)]
                lane_c = lax.broadcasted_iota(jnp.int32, (step, 128), 1)
                totals = [jnp.zeros((step, 128), f32) for _ in range(EXP_DEV)]
                for c in range(cols // 128):
                    here_g = slice(c * 128, c * 128 + 128)
                    here_u = slice(cols + c * 128, cols + c * 128 + 128)
                    gate, up, grad = pre[part, here_g], pre[part, here_u], mg[part, here_g]
                    sig = jax.nn.sigmoid(gate)
                    act = gate * sig
                    slope = sig * (1.0 + gate * (1.0 - sig))
                    middle = act * up
                    both_grad = middle * grad
                    factor = None
                    for x in reversed(range(EXP_DEV)):
                        low, high = max(x * ff, c * 128), min((x + 1) * ff, c * 128 + 128)
                        if low >= high:
                            continue
                        if high - low == 128:
                            totals[x] = totals[x] + both_grad
                            factor = w[x]
                        else:
                            inside = (lane_c >= low - c * 128) & (lane_c < high - c * 128)
                            totals[x] = totals[x] + jnp.where(inside, both_grad, 0.0)
                            factor = jnp.where(inside, w[x], 1.0 if factor is None else factor)
                    if factor is not None:
                        grad = grad * factor
                        middle = middle * factor
                    mid[part, here_g] = middle.astype(bf16)
                    pg[part, here_g] = (grad * up * slope).astype(bf16)
                    pg[part, here_u] = (grad * act).astype(bf16)
                sums = [jnp.sum(v, axis=1, keepdims=True) for v in totals]
                high = [v.astype(bf16).astype(f32) for v in sums]
                low = [v - w for v, w in zip(sums, high)]
                made = jnp.zeros((step, side), f32)
                for x in range(2):
                    made = jnp.where(lane == EXP_DEV * e + x, high[x], made)
                    made = jnp.where(lane == hot + EXP_DEV * e + x, low[x], made)
                aside[part, :] = made.astype(bf16)

            ov[...] = mm(mid[...], wd[...]).astype(bf16)
            for copy in out_copies(at, to, k):
                copy.start()

            @pl.when(u >= 2)
            def _():
                to_core(u).wait_send()

            back = mm(pg[...], wi[...]).astype(bf16)
            mine[(u // 4) % 2, u % 4, :, :D] = back[:rows]
            mine[(u // 4) % 2, u % 4, :, D:] = aside[:rows, :]
            stage[slot, :, :D] = back[rows:]
            stage[slot, :, D:] = aside[rows:, :]
            to_core(u).start()

        def chunk(i):
            return (1 + 2 * i) * (1 - i // 2) + 2 * (S - 1 - i) * (i // 2)

        def along(k):
            hop(2, k).start()
            hop(3, k).start()

        def pass_on(v):
            k = chunk(v // 4)

            @pl.when(v % 4 == 0)
            def _():
                hop(1, k).start()

            @pl.when(v % 4 == 1)
            def _():
                @pl.when((v == 1) | (k >= S // 2))
                def _():
                    hop(2, k).wait_recv()

                @pl.when(v == 1)
                def _():
                    diag(k, True).start()

                hop(4, k).start()

            @pl.when(v % 4 == 2)
            def _():
                @pl.when(k < S // 2)
                def _():
                    hop(3, k).wait_recv()

                hop(5, k).start()

            @pl.when(v % 4 == 3)
            def _():
                diag(k, True).wait_recv()
                hop(7, k).start()

        def to_diagonal(k):
            @pl.when(k < S // 2)
            def _():
                hop(2, k).wait_recv()
                diag(k, True).start()

            @pl.when(k >= S // 2)
            def _():
                hop(3, k).wait_recv()
                diag(k, False).start()

        z_copy(1).wait_send()
        z_copy(3).start()
        z_copy(1).wait_recv()
        along(1)
        hop(1, 1).start()
        for copy in weights:
            copy.wait()

        units = 4 * S

        @pl.loop(0, units)
        def _(u):
            i, g = u // 4, u % 4
            k = chunk(i)

            @pl.when(u > 0)
            def _():
                add_core(u - 1)

            @pl.when((i > 1) & (g == 0))
            def _():
                to_owner(i - 2).wait_send()

            @pl.when(i > 0)
            def _():
                j = i - 1

                @pl.when(g == 0)
                def _():
                    send_diagonals(j)

                @pl.when(g == 1)
                def _():
                    send_sides(j)

                @pl.when(g == 3)
                def _():
                    finish_sum(j)
                    to_owner(j).start()

            @pl.when((u > 0) & (u < units - 1))
            def _():
                pass_on(u + 1)

            @pl.when((g == 3) & (i < S - 1))
            def _():
                to_diagonal(chunk(i + 1))

            @pl.when((g == 1) & (i < S - 1))
            def _():
                later = chunk(i + 1)

                @pl.when(later > 0)
                def _():
                    z_copy(later).wait_send()

                    @pl.when(i == 0)
                    def _():
                        z_copy(2).start()

                    z_copy(later).wait_recv()

                along(later)

            for kind, at in ((1, 0), (4, 1), (5, 2), (7, 3)):
                @pl.when(g == at)
                def _(kind=kind):
                    hop(kind, k).wait_recv()

            at = e + (g % 2) * (ex - e) + (g // 2) * (ey - e)
            unit(at, flip(at, 1), k, u, u > 0)

            @pl.when(u == 0)
            def _():
                pass_on(1)

        last_sum = S - 1
        add_core(units - 1)
        send_diagonals(last_sum)
        weight_grads(1)
        results = [(dst, src) for src, dst in expert_rows(in_grad, down_grad, acc_in, acc_down)] + [
            (acc_down.at[pl.ds(both, shared)], sd_grad),
        ]
        last = [pltpu.make_async_copy(src, dst, fixed.at[1 + i]) for i, (src, dst) in enumerate(results)]
        for copy in last:
            copy.start()
        send_sides(last_sum)
        lane = lax.broadcasted_iota(jnp.int32, (shared, 128), 1)
        for n in range(D // 128):
            lanes = slice(n * 128, n * 128 + 128)
            gate, up = acc_in[both : both + shared, lanes], acc_in[cols + both : cols + both + shared, lanes]
            even = jnp.where(lane < 64, gate, pltpu.roll(up, 64, 1))
            odd = jnp.where(lane < 64, pltpu.roll(gate, 64, 1), up)
            for b, v in ((2 * n, even), (2 * n + 1, odd)):
                cut[b % S, b // S] = v.astype(bf16)
        handed = []
        for k in range(1, S):
            to = lax.rem(me + k, S)
            handed.append(
                remote(cut.at[to], sh_grad.at[me], sum_send.at[6 + S + k], sum_recv.at[6 + S + k], shard=to)
            )
        handed.append(pltpu.make_async_copy(cut.at[me], sh_grad.at[me], fixed.at[9]))
        for copy in handed:
            copy.start()
        last += handed
        for k in range(S):
            for kind in (1, 2, 3, 4, 5, 7):
                hop(kind, k).wait_send()
            diag(k, k < S // 2).wait_send()
        to_owner(last_sum - 1).wait_send()
        for w in (units - 2, units - 1):
            to_core(w).wait_send()
        for copy in out_copies(exy, flip(exy, 1), 0):
            copy.wait()
        finish_sum(last_sum)
        kept = pltpu.make_async_copy(mine.at[last_sum % 2, 0], back_sum.at[0], fixed.at[0])
        kept.start()
        for j in range(S - 1):
            to_owner(j).wait_recv()
        kept.wait()
        for copy in last:
            copy.wait()

    dma = pltpu.SemaphoreType.DMA
    shape = jax.ShapeDtypeStruct
    macs = 8 * S * rows * D * cols * 9
    return pl.pallas_call(
        kernel,
        out_shape=[
            shape((8, S, rows, wide), bf16),
            shape((8, S, rows, D), bf16),
            shape((S, rows, wide), bf16),
            shape(w_exp.shape, f32),
            shape(d_exp.shape, f32),
            shape((S, 8, shared, 128), bf16),
            shape((shared, D), f32),
        ],
        in_specs=[ANY] * 6,
        out_specs=[ANY] * 7,
        scratch_shapes=[
            pltpu.VMEM((2 * cols, D), bf16),
            pltpu.VMEM((cols, D), bf16),
            pltpu.VMEM((2 * cols, D), f32),
            pltpu.VMEM((cols, D), f32),
            pltpu.VMEM((2, T, wide), bf16),
            pltpu.VMEM((2, T, D), bf16),
            pltpu.VMEM((T, 2 * cols), f32),
            pltpu.VMEM((T, cols), f32),
            pltpu.VMEM((T, cols), bf16),
            pltpu.VMEM((T, 2 * cols), bf16),
            pltpu.VMEM((T, D), bf16),
            pltpu.VMEM((T, side), bf16),
            pltpu.VMEM((2, 4, rows, wide), bf16),
            pltpu.VMEM((2, rows, wide), bf16),
            pltpu.VMEM((2, rows, wide), bf16),
            pltpu.VMEM((2, rows // 2, wide), bf16),
            pltpu.VMEM((2, rows, wide), bf16),
            pltpu.VMEM((S, 8, shared, 128), bf16),
            dma((8, S)),
            dma((8, S)),
            dma((2, 2)),
            dma((2,)),
            dma((10,)),
            dma((6 + 2 * S,)),
            dma((6 + 2 * S,)),
        ],
        compiler_params=pltpu.CompilerParams(
            collective_id=ident, has_side_effects=True, vmem_limit_bytes=60 * 2**20
        ),
        cost_estimate=pl.CostEstimate(flops=2 * macs, bytes_accessed=10**8, transcendentals=10**6),
    )(h_side, cot_all, w_exp, w_sh, d_exp, d_sh)[1:]


def local(
    block_in,
    cotangent,
    doc_ids,
    routes,
    attn_gain,
    query_weight,
    kv_down_weight,
    kv_gain,
    kv_up_weight,
    out_weight,
    ffn_gain,
    router_weight,
    shared_in,
    shared_down,
    expert_in,
    expert_down,
):
    tok = block_in.shape[0]
    E, S = lax.axis_size("expert"), lax.axis_size("shard")
    e, s = lax.axis_index("expert"), lax.axis_index("shard")
    group = tok * S
    heads = HEADS // S
    units = SH_FF // (E * S)
    experts_all = EXP_DEV * E
    ff = expert_in.shape[2]
    first = s * tok
    scale = QK ** (-0.5)

    experts_cols = jnp.arange(experts_all, dtype=jnp.int32)

    def own(v):
        return lax.dynamic_slice_in_dim(v, first, tok, 0)

    def at_row(v, row):
        return jnp.pad(v, ((row, 16 + experts_all - row - v.shape[0]), (0, D // S - v.shape[1])))

    small = at_row(attn_gain[None], 0) + at_row(ffn_gain[None], 1) + at_row(kv_gain[None], 2)
    small = small + at_row(router_weight.T, 16)
    w_exp, d_exp = expert_in.transpose(0, 2, 1), expert_down.transpose(0, 2, 1)
    if KV_RANK // S // E >= 16:
        cot_all = lax.all_gather(cotangent, BOTH, axis=0, tiled=True)
        weights = [(query_weight, True), (kv_down_weight, False), (kv_up_weight, True)]
        x_rows, small, w_q, kv_down, kv_up = fetch_weights(0, E, S, block_in, small, weights)
    else:
        x_rows, small, w_q, kv_down, kv_up = shard_exchange(
            0,
            S,
            ("rows", block_in),
            ("rows", small),
            ("cols_to_rows", query_weight),
            ("rows", kv_down_weight),
            ("cols_to_rows", kv_up_weight),
        )
    small = small.reshape(S, 16 + experts_all, D // S)
    gain_a, gain_f = small[:, 0].reshape(D), small[:, 1].reshape(D)
    gain_k = small[:, 2, : KV_RANK // S].reshape(KV_RANK)
    router = small[:, 16:].transpose(1, 0, 2).reshape(experts_all, D)

    shared_in, shared_down, x_rows = lax.optimization_barrier((shared_in, shared_down, x_rows))
    rest = FF_PAD - EXP_DEV * ff
    if E == 8:
        sends = shared_rows(shared_in, S * units)
    else:
        sends = jnp.stack(
            [lax.dynamic_slice_in_dim(shared_in, at + e * S * units, S * units, 1).T for at in (0, SH_FF)]
        )
    sends = sends.reshape(2, S, units, D // S)
    w_sh = jnp.zeros((2, rest, D), bf16)
    for k in range(S):
        part = lax.dynamic_index_in_dim(sends, (s - k) % S, 1, keepdims=False)
        if k:
            part = lax.ppermute(part, "shard", [(i, (i - k) % S) for i in range(S)])
        w_sh = lax.dynamic_update_slice(w_sh, part, (0, 0, (s + k) % S * (D // S)))
    rows_here = shared_down.shape[0]
    holder = [i * S * units // rows_here for i in range(E)]

    def send_rows(to):
        at = jnp.clip((e * S + to) * units - s * rows_here, 0, rows_here - units)
        return lax.dynamic_slice_in_dim(shared_down, at, units, 0)

    mine = (e * S * units // rows_here) == s
    sh_down = jnp.where(mine, send_rows(s), 0)
    for k in range(1, S):
        pairs = [(i * S + holder[i], i * S + (holder[i] + k) % S) for i in range(E)]
        sh_down = sh_down + lax.ppermute(send_rows((s + k) % S), BOTH, pairs)

    d_sh = jnp.pad(sh_down, ((0, rest - units), (0, 0)))

    doc_row = doc_ids[0]
    cosine, sine = rope_tables(doc_row)
    index = jnp.arange(group, dtype=jnp.int32)
    allowed = (doc_row[:, None] == doc_row[None, :]) & (index[None, :] <= index[:, None])
    x_float = x_rows.astype(f32)
    scale_in = inv_rms(x_float)
    x_norm = (x_float * scale_in * gain_a).astype(bf16)
    query_raw = lax.optimization_barrier(mm(x_norm, w_q)).reshape(group, heads, QK)
    queries = jnp.concatenate(
        [
            query_raw[..., :NOPE],
            rotate(query_raw[..., NOPE:], cosine[:, None, :], sine[:, None, :]),
        ],
        axis=-1,
    ).astype(bf16)
    latent_raw = mm(x_norm, kv_down)
    compressed = latent_raw[:, :KV_RANK]
    scale_kv = inv_rms(compressed)
    latent = (compressed * scale_kv * gain_k).astype(bf16)
    key_rope = rotate(latent_raw[:, KV_RANK:], cosine, sine).astype(bf16)
    expanded = mm(latent, kv_up).astype(bf16).reshape(group, heads, NOPE + VDIM)
    keys = jnp.concatenate(
        [expanded[..., :NOPE], jnp.broadcast_to(key_rope[:, None, :], (group, heads, ROPE))], axis=-1
    )
    values = expanded[..., NOPE:]
    scores = jnp.einsum("qhd,khd->hqk", queries, keys, preferred_element_type=f32)
    scores = jnp.where(allowed[None], scores * scale, -jnp.inf)
    row_max = jnp.max(scores, axis=-1, keepdims=True)
    lse = row_max + jnp.log(jnp.sum(jnp.exp(scores - row_max), axis=-1, keepdims=True))
    probs = jnp.exp(scores - lse)
    probs_low = probs.astype(bf16)
    attended = (
        jnp.einsum("hqk,khd->qhd", probs_low, values, preferred_element_type=f32)
        .astype(bf16)
        .reshape(group, heads * VDIM)
    )
    attended, w_sh, d_sh = lax.optimization_barrier((attended, w_sh, d_sh))
    (resid_terms,) = shard_exchange(1, S, ("blocks", mm(attended, out_weight).astype(bf16)))

    resid = block_in.astype(f32) + jnp.sum(resid_terms.reshape(S, tok, D).astype(f32), axis=0)
    scale_ffn = inv_rms(resid)
    h_norm = (resid * scale_ffn * gain_f).astype(bf16)
    logits = mm_nt(h_norm, router)
    named = jnp.any(routes[:, :, None] == experts_cols[None, None, :], axis=1)
    masked = jnp.where(named, logits, -jnp.inf)
    top = jnp.exp(masked - jnp.max(masked, axis=-1, keepdims=True))
    route_w = top / jnp.sum(top, axis=-1, keepdims=True)
    w_high = route_w.astype(bf16)
    w_low = (route_w - w_high.astype(f32)).astype(bf16)
    side = -(-2 * experts_all // 128) * 128
    h_side = jnp.concatenate([h_norm, w_high, w_low, jnp.zeros((tok, side - 2 * experts_all), bf16)], axis=1)

    unit_at = slice(EXP_DEV * ff, EXP_DEV * ff + units)
    spot = (
        (e * EXP_DEV + jnp.arange(EXP_DEV, dtype=jnp.int32))[:, None] == experts_cols[None, :]
    ).astype(f32)

    def hidden_units(h_all, cot_all):
        count = h_all.shape[0]
        w_in = jnp.concatenate(
            [v for j in range(2) for v in (*w_exp[:, :, j * D : (j + 1) * D], w_sh[j])], axis=0
        )
        w_down = jnp.concatenate([*d_exp, d_sh], axis=0)
        w_all = h_all[:, D : D + experts_all].astype(f32) + h_all[:, D + experts_all : D + 2 * experts_all].astype(f32)
        w_cols = lax.dot_general(w_all, spot, (((1,), (1,)), ((), ())), precision=lax.Precision.HIGHEST)
        h_all = h_all[:, :D]
        weight = jnp.concatenate(
            [
                jnp.broadcast_to(w_cols[:, :1], (count, ff)),
                jnp.broadcast_to(w_cols[:, 1:], (count, ff)),
                jnp.ones((count, rest), f32),
            ],
            axis=1,
        )
        pre = mm_nt(h_all, w_in)
        gate_pre, up_pre = pre[:, :FF_PAD], pre[:, FF_PAD:]
        mid_grad = mm_nt(cot_all, w_down)
        sigmoid = jax.nn.sigmoid(gate_pre)
        act = gate_pre * sigmoid
        slope = sigmoid * (1.0 + gate_pre * (1.0 - sigmoid))
        mid = act * up_pre
        mid_low = (weight * mid).astype(bf16)
        weighted = weight * mid_grad
        gate_grad = (weighted * up_pre * slope).astype(bf16)
        up_grad = (weighted * act).astype(bf16)
        product = mid * mid_grad
        wg = jnp.stack([jnp.sum(product[:, k * ff : (k + 1) * ff], axis=1) for k in range(EXP_DEV)], axis=1)
        out_part = mm(mid_low, w_down).astype(bf16)
        pre_grad = jnp.concatenate([gate_grad, up_grad], axis=1)
        back_part = mm(pre_grad, w_in).astype(bf16)
        in_grad = jnp.stack(
            [
                jnp.concatenate([mm_tn(h_all, g[:, k * ff : (k + 1) * ff]) for g in (gate_grad, up_grad)], axis=0)
                for k in range(EXP_DEV)
            ]
        )
        down_grad = jnp.stack([mm_tn(cot_all, mid_low[:, k * ff : (k + 1) * ff]) for k in range(EXP_DEV)])
        sh_down_grad = mm_tn(mid_low[:, unit_at], cot_all)
        sh_in_grad = jnp.stack([mm_tn(g[:, unit_at], h_all) for g in (gate_grad, up_grad)])
        wg_all = lax.dot_general(wg, spot, (((1,), (0,)), ((), ())), precision=lax.Precision.HIGHEST)
        wg_high = wg_all.astype(bf16)
        wg_low = (wg_all - wg_high.astype(f32)).astype(bf16)
        back_part = jnp.concatenate(
            [back_part, wg_high, wg_low, jnp.zeros((count, side - 2 * experts_all), bf16)], axis=1
        )
        return ((in_grad, down_grad, sh_down_grad, sh_in_grad), (back_part, out_part))

    if E == 8:
        made = hidden_kernel(2, S, h_side, cot_all.reshape(E, S, tok, D), w_exp, w_sh, d_exp, d_sh, units)
        out_all, back_terms, expert_in_grad, expert_down_grad, sh_rows, shared_down_grad = made
        expert_in_grad, expert_down_grad = expert_in_grad.transpose(0, 2, 1), expert_down_grad.transpose(0, 2, 1)
        back_sum = jnp.sum(back_terms.astype(f32), axis=0)
    else:
        pieces = E // 8
        rows_in = [v.reshape(pieces, -1, v.shape[-1]) for v in (h_side, cotangent)]

        def one(total, rows):
            made, parts = hidden_units(*[lax.all_gather(v, BOTH, axis=0, tiled=True) for v in rows])
            sums = [lax.psum_scatter(v.astype(bf16), BOTH, scatter_dimension=0, tiled=True).astype(f32) for v in parts]
            return (jax.tree.map(jnp.add, total, made), sums)

        zeros = (
            jnp.zeros(expert_in.shape, f32),
            jnp.zeros(expert_down.shape, f32),
            jnp.zeros((units, D), f32),
            jnp.zeros((2, units, D), f32),
        )
        grads, sums = lax.scan(one, zeros, tuple(rows_in))
        back_sum, routed = [v.reshape(-1, v.shape[-1]) for v in sums]
        expert_in_grad, expert_down_grad, shared_down_grad, sh_in_grad = grads
    hidden_grad = back_sum[:, :D]
    weight_grad = back_sum[:, D : D + experts_all] + back_sum[:, D + experts_all : D + 2 * experts_all]

    logit_grad = (route_w * (weight_grad - jnp.sum(route_w * weight_grad, axis=-1, keepdims=True))).astype(bf16)
    router_grad = mm_tn(h_norm, logit_grad)
    hidden_grad = hidden_grad + mm(logit_grad, router)
    resid_part, ffn_gain_grad = norm_back(hidden_grad, resid, scale_ffn, gain_f)
    resid_grad = cotangent.astype(f32) + resid_part
    resid_low = resid_grad.astype(bf16)

    moves = [("rows", resid_low)]
    if E == 8:
        out_one, out_two, resid_rows = reduce_weights(4, E, S, [(out_all, 1), (out_all, 0)], moves)
        sh_rows, resid_rows = lax.optimization_barrier((sh_rows, resid_rows))
        sh_rows = sh_rows.transpose(1, 0, 2, 3)
    else:
        (resid_rows,) = shard_exchange(4, S, *moves)
        sh_sends = sh_in_grad.astype(bf16).reshape(2 * units, E * S, D // (E * S)).transpose(1, 0, 2)
        sh_rows = lax.all_to_all(sh_sends, BOTH, split_axis=0, concat_axis=0, tiled=True)
        shared_in_grad = (
            sh_rows.reshape(E * S, 2, units, D // (E * S))
            .transpose(3, 1, 0, 2)
            .reshape(D // (E * S), 2 * SH_FF)
            .astype(f32)
        )
    att_grad = mm_nt(resid_rows, out_weight).astype(bf16).reshape(group, heads, VDIM)
    out_grad = mm_tn(attended, resid_rows)

    values_grad = jnp.einsum("hqk,qhd->khd", probs_low, att_grad, preferred_element_type=f32)
    probs_grad = jnp.einsum("qhd,khd->hqk", att_grad, values, preferred_element_type=f32)
    delta = jnp.sum(probs * probs_grad, axis=-1, keepdims=True)
    score_grad = lax.optimization_barrier((probs * (probs_grad - delta) * scale).astype(bf16))
    q_grad = jnp.einsum("hqk,khd->qhd", score_grad, keys, preferred_element_type=f32)
    k_grad = jnp.einsum("hqk,qhd->khd", score_grad, queries, preferred_element_type=f32)
    rope_part = jnp.sum(k_grad[..., NOPE:], axis=1)
    key_grad = (
        jnp.concatenate([k_grad[..., :NOPE], values_grad], axis=-1)
        .reshape(group, heads * (NOPE + VDIM))
        .astype(bf16)
    )
    query_grad = (
        jnp.concatenate(
            [q_grad[..., :NOPE], unrotate(q_grad[..., NOPE:], cosine[:, None, :], sine[:, None, :])], axis=-1
        )
        .reshape(group, heads * QK)
        .astype(bf16)
    )
    latent_part = jnp.concatenate([mm_nt(key_grad, kv_up), rope_part, jnp.zeros((group, ROPE), f32)], axis=1)
    norm_part = mm_nt(query_grad, w_q)
    (latent_back,) = shard_exchange(5, S, ("blocks", latent_part.astype(bf16)))
    norm_low = norm_part.astype(bf16)
    latent_back = jnp.sum(latent_back.reshape(S, tok, -1).astype(f32), axis=0)
    compressed_grad, kv_gain_grad = norm_back(latent_back[:, :KV_RANK], own(compressed), own(scale_kv), gain_k)
    latent_grad = jnp.concatenate(
        [compressed_grad, unrotate(latent_back[:, KV_RANK : KV_RANK + ROPE], own(cosine), own(sine))], axis=1
    ).astype(bf16)
    norm_own = mm_nt(latent_grad, kv_down)
    x_own, scale_x = block_in.astype(f32), own(scale_in)
    attn_gain_grad = jnp.sum(norm_part * x_float * scale_in, axis=0) + jnp.sum(norm_own * x_own * scale_x, axis=0)

    rows, kv_rows = D // (E * S), KV_RANK // (E * S)
    q_w_grad = mm_tn(x_norm, query_grad)
    kv_up_grad = mm_tn(latent, key_grad)
    (latent_grad_rows,) = shard_exchange(6, S, ("rows", latent_grad))
    x_cols = lax.dynamic_slice_in_dim(x_norm, s * (D // S), D // S, 1)
    kv_down_grad = mm_tn(x_cols, latent_grad_rows)
    def lanes(v, *more):
        v = v.reshape((E, S, 1, -1)) if v.ndim == 1 else v
        if more:
            v = jnp.concatenate([v, more[0].reshape(E, S, 1, -1)], axis=-1)
        return jnp.pad(v, ((0, 0), (0, 0), (0, 0), (0, 128 - v.shape[-1])))

    gains = jnp.concatenate(
        [
            lanes(attn_gain_grad, kv_gain_grad),
            lanes(ffn_gain_grad),
            lanes(router_grad.reshape(E, S, rows, experts_all).transpose(0, 1, 3, 2)),
        ],
        axis=2,
    ).astype(bf16)
    gain_count = -(-gains.shape[2] // 8) * 8
    gains = jnp.pad(gains, ((0, 0), (0, 0), (0, gain_count - gains.shape[2]), (0, 0))).reshape(E, S * gain_count, 128)

    def cut(g):
        return g.astype(bf16).reshape(E, g.shape[0] // E, g.shape[1])

    q_parts, up_parts, out_parts, down_parts = cut(q_w_grad), cut(kv_up_grad), cut(out_grad), cut(kv_down_grad)
    if E == 8:
        (
            out_three,
            out_four,
            query_weight_grad,
            mine_out,
            kv_up_weight_grad,
            mine_down,
            gain_sums,
            norm_terms,
            sh_rows,
        ) = reduce_weights(
            7,
            E,
            S,
            [
                (out_all, 2),
                (out_all, 3),
                (q_parts, "rows_to_cols"),
                (out_parts, "keep"),
                (up_parts, "rows_to_cols"),
                (down_parts, "keep"),
                (gains, "rows"),
            ],
            [("blocks", norm_low), ("plane", sh_rows)],
        )
        sh_rows = sh_rows.reshape(E * S * units, -1).T
        shared_in_grad = jnp.concatenate([sh_rows[: D // (E * S)], sh_rows[D // (E * S) :]], axis=1).astype(f32)
        routed = sum(v.astype(f32) for v in (out_one, out_two, out_three, out_four))
    else:
        sums = [
            lax.psum_scatter(v, "expert", scatter_dimension=0, tiled=False)
            for v in (gains, down_parts, out_parts, q_parts, up_parts)
        ]
        gain_sums, mine_down, mine_out = lax.all_gather(sums[0], "shard", axis=0, tiled=True), sums[1], sums[2]
        query_weight_grad, kv_up_weight_grad = [
            lax.all_to_all(v, "shard", split_axis=0, concat_axis=1, tiled=True) for v in sums[3:]
        ]
        (norm_terms,) = shard_exchange(7, S, ("blocks", norm_low))
    pairs = [(ee * S + ss, E * ss + ee) for ee in range(E) for ss in range(S)]
    out_weight_grad = lax.ppermute(mine_out, BOTH, pairs).astype(f32)
    kv_down_weight_grad = lax.ppermute(mine_down, BOTH, pairs).astype(f32)
    block_out = resid + routed
    gain_sums = gain_sums.reshape(S, S, gain_count, 128)
    gain_sums = lax.dynamic_index_in_dim(gain_sums, s, 1, keepdims=False)
    gain_sums = jnp.sum(gain_sums.astype(f32), axis=0)
    norm_grad = norm_own + jnp.sum(norm_terms.reshape(S, tok, D).astype(f32), axis=0)
    scaled = norm_grad * gain_a
    input_grad = resid_grad + (
        scale_x * scaled - x_own * scale_x**3 * jnp.mean(scaled * x_own, axis=-1, keepdims=True)
    )

    return (
        block_out,
        input_grad,
        gain_sums[0, :rows],
        query_weight_grad.astype(f32),
        kv_down_weight_grad,
        gain_sums[0, rows : rows + kv_rows],
        kv_up_weight_grad.astype(f32),
        out_weight_grad,
        gain_sums[1, :rows],
        gain_sums[2 : 2 + experts_all, :rows].T,
        shared_in_grad,
        shared_down_grad,
        expert_in_grad,
        expert_down_grad,
    )


def solution(mesh):
    tokens = P(BOTH, None)
    shard = P("shard", None)
    in_specs = (
        tokens,
        tokens,
        P("expert", None),
        tokens,
        P("shard"),
        shard,
        shard,
        P("shard"),
        shard,
        shard,
        P("shard"),
        shard,
        shard,
        shard,
        P("expert", None, "shard"),
        P("expert", None, "shard"),
    )
    out_specs = (
        tokens,
        tokens,
        P(BOTH),
        tokens,
        tokens,
        P(BOTH),
        tokens,
        tokens,
        P(BOTH),
        tokens,
        tokens,
        tokens,
        P("expert", None, "shard"),
        P("expert", None, "shard"),
    )
    return jax.shard_map(local, mesh=mesh, in_specs=in_specs, out_specs=out_specs, check_vma=False)
```

time: 1470 us -> 810 us (0.55)
  Pallas kernels: 0 us -> 609 us
  waiting for transfers between devices: 539 us -> 11 us
  blocking collectives: 279 us -> 0 us
  matrix products: 309 us -> 42.6 us
  local copies, waits for them, and re-layouts: 151 us -> 64.4 us
  starting transfers between devices: 87.9 us -> 13.5 us
  other arithmetic: 84.9 us -> 44.6 us
    pallas_call x0 -> x8, Pallas kernels: none -> 609 us  [the longest x1 264 us: hidden_kernel(): pl.pallas_call(kernel, out_shape=[shape((8, S, rows, wide), bf16), shape(...]
    ppermute x49 -> x8, waiting for transfers between devices: 282 us -> 10.4 us  [the longest x3 10.4 us: local(): part = lax.ppermute(part, 'shard', [(i, (i - k) % S) for i in range(S)])]
    dot_general x27 -> x15, matrix products: 281 us -> 36 us  [dot(): return lax.dot_general(a, b, (dims, ((), ())), preferred_element_type=f32)]
    all_gather x6 -> x0, blocking collectives: 239 us -> none  [gather(): return lax.all_gather(v, 'shard', axis=0, tiled=True)]
    unnamed x17 -> x1, waiting for transfers between devices: 132 us -> 0.68 us
    all_to_all x10 -> x0, waiting for transfers between devices: 79.3 us -> none  [the longest x4 73.3 us: columns_to_heads(): lax.all_to_all(parts, 'shard', split_axis=1, concat_axis=0, tiled=True)]
    all_to_all x10 -> x0, starting transfers between devices: 51.8 us -> none  [the longest x3 20.8 us: scatter_columns(): lax.all_to_all(mine.reshape(S, rows // (E * S), cols), 'shard', split_axi...]
    unnamed x1 -> x0, blocking collectives: 40.5 us -> none
  transfers between devices with their start and end apart: 74 -> 9, of which waited for: 27 -> 1; matrix products, arithmetic and copies ran while one was open for 25% -> 9% of each run, Pallas kernels for 0% -> 19%
where the time goes in v2:
time: 810 us; the launch traced here: 801 us
  Pallas kernels  609 us (75%)
  local copies, waits for them, and re-layouts  64.4 us (8%)
  other arithmetic  44.6 us (6%)
  matrix products  42.6 us (5%)
  between operations  15.9 us (2%)
  starting transfers between devices  13.5 us (2%)
  waiting for transfers between devices  11 us (1%)
    pallas_call x1, Pallas kernels, hidden_kernel(): pl.pallas_call(kernel, out_shape=[shape((8, S, rows, wide), bf16), shape(...  264 us
    pallas_call x2, Pallas kernels, reduce_weights(): pl.pallas_call(kernel, out_shape=[jax.ShapeDtypeStruct(out_shape(a, kind)...  153 us
    pallas_call x1, Pallas kernels, fetch_weights(): pl.pallas_call(kernel, out_shape=[jax.ShapeDtypeStruct((S * v.shape[0], v...  108 us
    pallas_call x3, Pallas kernels, shard_exchange(): pl.pallas_call(kernel, out_shape=[jax.ShapeDtypeStruct(exchange_shape(kin...  82.2 us
    dot_general x15, matrix products, dot(): return lax.dot_general(a, b, (dims, ((), ())), preferred_element_type=f32)  36 us
    unnamed x173, local copies, waits for them, and re-layouts  32.7 us
  transfers between devices with their start and end apart: 9, of which 1 were waited for; matrix products, arithmetic and copies ran while one was open for 9% of the time, Pallas kernels for 19%

profile of v2, /device:TPU:0, one launch (start us, length us, event | category | flops | bytes accessed | tf_op | source)
XLA Modules:
  0.0 800.5 jit_solution(15497767027097683418)
XLA Ops:
  9.4 2.1 copy.155
  12.8 108.5 %shard_map.263 = (bf16[512,2048]{1,0:T(8,128)(2,1)}, bf16[128,512]{1,0:T(8,128)(2,1)}, bf16[4,4,2,64,768]{4,3,2,1,0:T(8,128)(2,1)}, bf16[4,4,2,64,576]{4,3,2,1,0:T(8,128)(2,1)}, bf16[4,4,2,16,1024]{4,3,2,1,0:T(8,128)(2,1)}) custom-call(bf16[128,2048]{1,0:T(8,128)(2,1)} %refs_0_.1, bf16[32,512]{1,0:T(8,128)(2,1)} %pad_add_fusion.refs_1_, ...), custom_call_target="tpu_custom_call" | custom-call | tf_op jit(solution)/shard_map/pallas_call | solution.py:251
  121.4 2.6 copy-done.1
  128.5 2.4 constant_dynamic-slice_fusion.2
  130.9 3.5 collective-permute-start.3
  134.4 2.5 collective-permute-start.5
  136.8 2.6 collective-permute-start.4
  139.6 2.2 fusion.1
  153.3 2.4 fusion.57
  156.4 2.9 convolution_convert_fusion.5
  159.4 2.3 copy.197
  162.7 5.8 fusion.61
  168.5 3.1 copy.158
  178.9 2.2 convolution_convert_fusion.8
  187.2 10.3 %collective-permute-done.2 = bf16[2,88,512]{2,1,0:T(8,128)(2,1)S(1)} collective-permute-done((bf16[2,88,512]{2,1,0:T(8,128)(2,1)S(1)}, bf16[2,88,512]{2,1,0:T(8,128)(2,1)S(1)}, u32[]{:S(2)}, u32[]{:S(2)}) %collective-permute-start.2) | collective-permute-done | bytes 180256 | tf_op jit(solution)/shard_map/ppermute | solution.py:1016
  200.9 3.7 convolution_convert_fusion.2.refs_0_
  204.5 39.2 %shard_map.265 = bf16[512,2048]{1,0:T(8,128)(2,1)} custom-call(bf16[512,2048]{1,0:T(8,128)(2,1)} %convolution_convert_fusion.2.refs_0_), custom_call_target="tpu_custom_call" | custom-call | tf_op jit(solution)/shard_map/pallas_call | solution.py:147
  243.7 2.1 convert_reduce_fusion.2
  249.9 263.7 %shard_map.266 = (bf16[8,4,128,2176]{3,2,1,0:T(8,128)(2,1)}, bf16[8,4,128,2048]{3,2,1,0:T(8,128)(2,1)}, bf16[4,128,2176]{2,1,0:T(8,128)(2,1)}, f32[2,352,4096]{2...) custom-call(bf16[128,2176]{1,0:T(8,128)(2,1)} %concatenate.46.h_ref, ...), custom_call_target="tpu_custom_call" | custom-call | flops 135291469824 | bytes 100000000 | tf_op jit(solution)/shard_map/pallas_call | solution.py:897
  518.5 53.5 %shard_map.267 = (bf16[128,2048]{1,0:T(8,128)(2,1)S(1)}, bf16[128,2048]{1,0:T(8,128)(2,1)S(1)}, bf16[512,2048]{1,0:T(8,128)(2,1)S(1)}) custom-call(bf16[8,4,128,2048]{3,2,1,0:T(8,128)(2,1)} %get-tuple-element.56.refs_0_, bf16[128,2048]{1,0:T(8,128)(2,1)S(1)} %get-tuple-element.84.refs_1_), custom_call_target="tpu_custom_call" | custom-call | tf_op jit(solution)/shard_map/pallas_call | solution.py:469
  573.5 2.6 convolution_convert_fusion.1
  578.2 3.3 multiply_convert_fusion
  588.8 4.4 fusion.56
  593.2 3.5 convolution_convert_fusion
  601.2 25.0 %shard_map.268 = bf16[512,640]{1,0:T(8,128)(2,1)} custom-call(bf16[512,640]{1,0:T(8,128)(2,1)} %maximum_maximum_fusion.refs_0_), custom_call_target="tpu_custom_call" | custom-call | tf_op jit(solution)/shard_map/pallas_call | solution.py:147
  631.4 18.1 %shard_map.269 = bf16[512,576]{1,0:T(8,128)(2,1)} custom-call(bf16[128,576]{1,0:T(8,128)(2,1)} %pad_maximum_fusion.6.refs_0_), custom_call_target="tpu_custom_call" | custom-call | tf_op jit(solution)/shard_map/pallas_call | solution.py:147
  649.5 3.8 fusion.16
  653.8 2.6 convolution_convert_fusion.6
  660.7 99.6 %shard_map.270 = (bf16[128,2048]{1,0:T(8,128)(2,1)S(1)}, bf16[128,2048]{1,0:T(8,128)(2,1)S(1)}, bf16[64,3072]{1,0:T(8,128)(2,1)S(1)}, bf16[64,2048]{1,0:T(8,128)...) custom-call(bf16[8,4,128,2048]{3,2,1,0:T(8,128)(2,1)} %get-tuple-ele, ...), custom_call_target="tpu_custom_call" | custom-call | tf_op jit(solution)/shard_map/pallas_call | solution.py:469
  767.9 2.2 convert_reduce_fusion.1
  780.4 10.2 %copy.219 = f32[2,4096,352]{1,2,0:T(8,128)} copy(f32[2,4096,352]{1,2,0:T(8,128)} %bitcast.129) | data formatting | bytes 23068672
  790.7 2.5 copy.220
  (287 shorter events, 89.2 us)
Async XLA Ops:
  7.2 193.7 %copy-start = (bf16[512,2048]{1,0:T(8,128)(2,1)S(1)}, bf16[512,2048]{1,0:T(8,128)(2,1)}, u32[]{:S(2)}) copy-start(bf16[512,2048]{1,0:T(8,128)(2,1)} %param.25) | copy-start | bytes 6291460
  7.2 242.8 %all-gather.2.cloned.1.call-start = ((), (), s32[]{:S(2)}) async-start(), calls=%async_computation | async-start | bytes 17301504 | tf_op jit(solution)/shard_map/all_gather | solution.py:985
  124.9 14.5 %copy-start.65 = (s32[1,512]{1,0:T(1,128)S(1)}, s32[1,512]{1,0:T(1,128)}, u32[]{:S(2)}) copy-start(s32[1,512]{1,0:T(1,128)} %param.18) | copy-start | bytes 6148
  125.8 59.8 %collective-permute-start.1 = (bf16[2,88,512]{2,1,0:T(8,128)(2,1)}, bf16[2,88,512]{2,1,0:T(8,128)(2,1)}, u32[]{:S(2)}, u32[]{:S(2)}) collective-permute-start(bf16[2,88,512]{2,1,0:T(8,128)(2,1)} %get-tuple-element.106), channel_id=1, source_target_pairs={{0,2},{1,3},{2,0},{3,1},{4,6},{5,7},{6,4},{7,5},{8,10},{9,11},{10,... | collective-permute-start | bytes 540680 | tf_op jit(solution)/shard_map/ppermute | solution.py:1016
  127.1 56.9 %collective-permute-start = (bf16[2,88,512]{2,1,0:T(8,128)(2,1)}, bf16[2,88,512]{2,1,0:T(8,128)(2,1)}, u32[]{:S(2)}, u32[]{:S(2)}) collective-permute-start(bf16[2,88,512]{2,1,0:T(8,128)(2,1)} %get-tuple-element.107), channel_id=1, source_target_pairs={{0,3},{1,0},{2,1},{3,2},{4,7},{5,4},{6,5},{7,6},{8,11},{9,8},{10,9... | collective-permute-start | bytes 540680 | tf_op jit(solution)/shard_map/ppermute | solution.py:1016
  130.9 67.4 %collective-permute-start.3 = (bf16[88,2048]{1,0:T(8,128)(2,1)}, bf16[88,2048]{1,0:T(8,128)(2,1)}, u32[]{:S(2)}, u32[]{:S(2)}) collective-permute-start(bf16[88,2048]{1,0:T(8,128)(2,1)} %get-tuple-element.90), channel_id=1, source_target_pairs={{0,1},{4,5},{9,10},{13,14},{18,19},{22,23},{27,24},{31,28}} | collective-permute-start | bytes 1081352 | tf_op jit(solution)/shard_map/ppermute | solution.py:1029
  134.4 63.9 %collective-permute-start.5 = (bf16[88,2048]{1,0:T(8,128)(2,1)}, bf16[88,2048]{1,0:T(8,128)(2,1)}, u32[]{:S(2)}, u32[]{:S(2)}) collective-permute-start(bf16[88,2048]{1,0:T(8,128)(2,1)} %get-tuple-element.91), channel_id=1, source_target_pairs={{0,3},{4,7},{9,8},{13,12},{18,17},{22,21},{27,26},{31,30}} | collective-permute-start | bytes 1081352 | tf_op jit(solution)/shard_map/ppermute | solution.py:1029
  136.8 61.5 %collective-permute-start.4 = (bf16[88,2048]{1,0:T(8,128)(2,1)}, bf16[88,2048]{1,0:T(8,128)(2,1)}, u32[]{:S(2)}, u32[]{:S(2)}) collective-permute-start(bf16[88,2048]{1,0:T(8,128)(2,1)} %get-tuple-element.92), channel_id=1, source_target_pairs={{0,2},{4,6},{9,11},{13,15},{18,16},{22,20},{27,25},{31,29}} | collective-permute-start | bytes 1081352 | tf_op jit(solution)/shard_map/ppermute | solution.py:1029
  143.3 3.4 copy-start.32
  149.7 9.6 %copy-start.41 = (f32[512,32]{1,0:T(8,128)}, f32[512,32]{1,0:T(8,128)S(1)}, u32[]{:S(2)}) copy-start(f32[512,32]{1,0:T(8,128)S(1)} %get-tuple-element.115) | copy-start | bytes 196612
  149.7 9.6 %copy-start.42 = (f32[512,32]{1,0:T(8,128)}, f32[512,32]{1,0:T(8,128)S(1)}, u32[]{:S(2)}) copy-start(f32[512,32]{1,0:T(8,128)S(1)} %get-tuple-element.118) | copy-start | bytes 196612
  149.8 24.3 %copy-start.50 = (f32[512,32]{0,1:T(8,128)}, f32[512,32]{0,1:T(8,128)S(1)}, u32[]{:S(2)}) copy-start(f32[512,32]{0,1:T(8,128)S(1)} %copy.160) | copy-start | bytes 196612
  155.7 25.4 %copy-start.66 = (f32[512]{0:T(512)}, f32[512]{0:T(512)S(1)}, u32[]{:S(2)}) copy-start(f32[512]{0:T(512)S(1)} %add_rsqrt_fusion) | copy-start | bytes 6148
  156.4 5.2 copy-start.62
  162.7 13.0 %copy-start.36 = (bf16[512,4,128]{0,2,1:T(8,128)(2,1)}, bf16[512,4,128]{0,2,1:T(8,128)(2,1)S(1)}, u32[]{:S(2)}) copy-start(bf16[512,4,128]{0,2,1:T(8,128)(2,1)S(1)} %slice.136) | copy-start | bytes 1572868
  174.2 3.6 copy-start.45
  178.9 3.5 copy-start.61
  178.9 3.7 copy-start.48
  178.9 5.1 copy-start.58
  184.0 13.6 %collective-permute-start.2 = (bf16[2,88,512]{2,1,0:T(8,128)(2,1)S(1)}, bf16[2,88,512]{2,1,0:T(8,128)(2,1)S(1)}, u32[]{:S(2)}, u32[]{:S(2)}) collective-permute-start(bf16[2,88,512]{2,1,0:T(8,128)(2,1)S(1)} %copy-done.58), channel_id=1, source_target_pairs={{0,1},{1,2},{2,3},{3,0},{4,5},{5,6},{6,7},{7,4},{8,9},{9,10},{10,1... | collective-permute-start | bytes 540680 | tf_op jit(solution)/shard_map/ppermute | solution.py:1016
  246.1 270.8 %copy-start.15 = (f32[128,2048]{1,0:T(8,128)}, f32[128,2048]{1,0:T(8,128)S(1)}, u32[]{:S(2)}) copy-start(f32[128,2048]{1,0:T(8,128)S(1)} %get-tuple-element.87) | copy-start | bytes 3145732
  588.8 4.4 copy-start.33
  599.1 29.4 %copy-start.64 = (f32[4,1,128]{2,1,0:T(1,128)S(1)}, f32[4,1,128]{2,1,0:T(1,128)}, u32[]{:S(2)}) copy-start(f32[4,1,128]{2,1,0:T(1,128)} %copy-done.62) | copy-start | bytes 6148
  599.1 29.4 %copy-start.75 = (f32[128]{0:T(128)S(1)}, f32[128]{0:T(128)}, u32[]{:S(2)}) copy-start(f32[128]{0:T(128)} %get-tuple-element.83) | copy-start | bytes 1540
  599.2 30.4 %copy-start.78 = (f32[128]{0:T(128)S(1)}, f32[128]{0:T(128)}, u32[]{:S(2)}) copy-start(f32[128]{0:T(128)} %get-tuple-element.82) | copy-start | bytes 1540
  626.2 23.3 %copy-start.73 = (f32[128]{0:T(128)S(1)}, f32[128]{0:T(128)}, u32[]{:S(2)}) copy-start(f32[128]{0:T(128)} %get-tuple-element.129) | copy-start | bytes 1540
  649.5 3.9 copy-start.72
  764.2 13.9 %collective-permute-start.6 = (bf16[64,576]{1,0:T(8,128)(2,1)S(1)}, bf16[64,576]{1,0:T(8,128)(2,1)S(1)}, u32[]{:S(2)}, u32[]{:S(2)}) collective-permute-start(bf16[64,576]{1,0:T(8,128)(2,1)S(1)} %get-tuple-element.69), channel_id=1, source_target_pairs={{0,0},{1,8},{2,16},{3,24},{4,1},{5,9},{6,17},{7,25},{8,2},{9,10},{... | collective-permute-start | bytes 221192 | tf_op jit(solution)/shard_map/ppermute | solution.py:1291
  764.8 13.9 %collective-permute-start.7 = (bf16[64,2048]{1,0:T(8,128)(2,1)}, bf16[64,2048]{1,0:T(8,128)(2,1)S(1)}, u32[]{:S(2)}, u32[]{:S(2)}) collective-permute-start(bf16[64,2048]{1,0:T(8,128)(2,1)} %get-tuple-element.71), channel_id=1, source_target_pairs={{0,0},{1,8},{2,16},{3,24},{4,1},{5,9},{6,17},{7,25},{8,2},{9,10},{... | collective-permute-start | bytes 786440 | tf_op jit(solution)/shard_map/ppermute | solution.py:1290
  775.3 4.3 copy-start.49
  778.7 11.9 %slice-start = ((s8[5767168]{0:T(1024)(128)(4,1)}), s8[4194304]{0:T(1024)(128)(4,1)S(1)}, s32[]{:S(2)}) async-start(s8[5767168]{0:T(1024)(128)(4,1)} %bitcast.131), calls=%async_computation.1 | async-start | bytes 8388608
  780.4 10.3 %slice-start.1 = ((s8[5767168]{0:T(1024)(128)(4,1)}), s8[1572864]{0:T(1024)(128)(4,1)S(1)}, s32[]{:S(2)}) async-start(s8[5767168]{0:T(1024)(128)(4,1)} %bitcast.131), calls=%async_computation.2 | async-start | bytes 3145728
  (60 other events, 109.7 us)
Sparse Core Ops, SparseCore 0:
  11.0 187.2 all-gather.1
